TPU v7x, 32 devices: a whole 2x2x4 slice. The times are simulated.
32 devices in a mesh: grp: 2 (over y), row: 4 (over z), col: 2 (over x), rep: 2 (over core).
Axes of the slice: x: 2, y: 2, z: 4, core: 2. Of those that a mesh axis runs over, the one named last changes fastest.
Arguments:
- emb_row: bfloat16 [2048, 1280], P(('grp', 'row', 'rep'), 'col'), parts along dimension 0, may hold values from -6 to 6
- emb_col: bfloat16 [512, 1280], P(('grp', 'col'), 'row'), parts along dimension 0, may hold values from -6 to 6
- proj_row: bfloat16 [1280, 64], replicated, may hold values from -0.15625 to 0.15625
- proj_col: bfloat16 [1280, 64], replicated, may hold values from -0.15625 to 0.15625
- pair_out: bfloat16 [64, 64], replicated, may hold values from -0.75 to 0.75
- pair_bias: float32 [64], replicated, may hold values from -3 to 3
- conv_weight: bfloat16 [3, 3, 64, 64], replicated, may hold values from -0.25 to 0.25
- conv_bias: float32 [64], replicated, may hold values from -3 to 3
- target: bfloat16 [64, 2048, 256], P(None, ('grp', 'row', 'rep'), 'col'), parts along dimension 1, may hold values from -6 to 6
- kept_tiles: int32 [16, 2], P(('grp', 'row', 'rep'), 'col'), parts along dimension 0, may hold values 0 or 1
Outputs:
- cell_loss: float32 [2048, 256], P(('grp', 'row', 'rep'), 'col'), parts along dimension 0
- grad_conv: float32 [6, 3, 64, 64], P('grp'), parts along dimension 0
- grad_bias: float32 [128], P('grp'), parts along dimension 0
There are 2 independent parts, one for each index of `grp`. A program takes and returns all parts, laid end to end along the dimension named above; an argument that names none is the same for every part. Nothing has to cross between parts.
All inputs are finite; a program needn't handle non-finite values. No bound on the sum of `kept_tiles` on one device may be relied on, other than what follows from the above.
Results may differ from a plain program's by a relative error of at most 0.0025.
Values may be sent and summed in bfloat16 or wider, within the bound.
No kernel may reach another device: no remote copies, remote signals or barrier semaphores. Data moves between devices by JAX's collectives and lax.ppermute only.
A program may use at most 128 MiB of HBM per device.

v0:
```python
import functools

import jax
import jax.numpy as jnp
from jax import lax
from jax.experimental import pallas as pl
from jax.experimental.pallas import tpu as pltpu
from jax.sharding import PartitionSpec as P

REACH = 2
F32 = jnp.float32
BF16 = jnp.bfloat16
ROWS_BY_COLS = (((1,), (1,)), ((), ()))
MESH = ("row", "col", "rep")


def swap(x, row=0, col=0, rep=0):
    sizes = [lax.axis_size(axis) for axis in MESH]

    def index(r, c, p):
        return (r * sizes[1] + c) * sizes[2] + p

    places = [(r, c, p) for r in range(sizes[0]) for c in range(sizes[1]) for p in range(sizes[2])]
    return lax.ppermute(
        x, MESH, [(index(r, c, p), index(r ^ row, c ^ col, p ^ rep)) for r, c, p in places]
    )


def steps(axis, first=1):
    step = first
    while step < lax.axis_size(axis):
        yield step
        step *= 2


def zeros_kernel(zeros_ref):
    zeros_ref[...] = jnp.zeros_like(zeros_ref)


def project_kernel(
    zeros_ref, kept_ref, row_ref, row_proj_ref, col_ref, col_proj_ref,
    col_send_ref, row_send_ref, cross_send_ref, col_wide, *, sliced
):
    row_at = col_at = 0
    depth = row_ref.shape[1]
    if sliced[0]:
        row_at = pl.multiple_of(lax.axis_index("col") * depth, 128)
    if sliced[1]:
        col_at = pl.multiple_of(lax.axis_index("row") * col_ref.shape[0], 16)
    col_wide[...] = jnp.zeros_like(col_wide)
    col_wide[pl.ds(col_at, col_ref.shape[0]), :] = col_ref[...]
    half, wide = row_ref.shape[0] // 2, 2 * row_proj_ref.shape[0]
    lane = lax.broadcasted_iota(jnp.int32, (REACH, wide), 1)

    def packed(x):
        return jnp.concatenate([x[:half], x[half:]], axis=1)

    def ends(x):
        return jnp.where(lane < wide // 2, x[:REACH], x[half - REACH:])

    kept = jnp.broadcast_to(kept_ref[...].astype(F32), (1, wide))
    rows = packed(
        lax.dot_general(
            row_ref[...], row_proj_ref[:, pl.ds(row_at, depth)], ROWS_BY_COLS, preferred_element_type=F32
        )
    )
    cols = packed(jnp.dot(col_proj_ref[...], col_wide[...], preferred_element_type=F32).T)
    row_ends, col_ends = ends(rows), ends(cols)
    zero = zeros_ref[...]
    col_send_ref[0:half, :] = rows
    row_send_ref[0:half, :] = cols
    col_send_ref[half:, :] = jnp.concatenate([col_ends, kept, zero[:5]], axis=0)
    row_send_ref[half:, :] = jnp.concatenate([row_ends, kept, zero[:5]], axis=0)
    cross_send_ref[...] = jnp.concatenate([row_ends, kept, col_ends, zero[:3]], axis=0)


def tile_kernel(
    row_ref, col_ref, misc_ref, out_ref, pbias_ref, weight_ref, cbias_ref, target_hbm,
    loss_ref, grad_ref, target_ref, sem, hid, dif_taps, feat, rhs, near, far, bias_sum, *, norm
):
    chans, rows, cols = target_ref.shape
    half, wide = row_ref.shape
    rank = wide // 2
    width = 2 * cols
    pairs = rows // 2 + 2
    taps = weight_ref.shape[0]

    target_copy = pltpu.make_async_copy(target_hbm, target_ref, sem)
    target_copy.start()

    rhs[...] = jnp.zeros_like(rhs)
    lane = lax.broadcasted_iota(jnp.int32, (half, wide), 1)
    for start, value in ((0, col_ref[...]), (cols, misc_ref[0:REACH, :])):
        turned = pltpu.roll(value, rank, 1)
        size = value.shape[0]
        lower = lane[:size] < rank
        gap = half if start == 0 else cols - REACH
        for base, first, last in ((0, value, turned), (2 * cols, turned, value)):
            keep_half = lower if base == 0 else ~lower
            at = base + start
            rhs[at:at + size, :] = jnp.where(keep_half, first, 0.0)
            rhs[at + gap:at + gap + size, :] = jnp.where(keep_half, last, 0.0)
    factors = rhs[...].astype(BF16)

    lane = lax.broadcasted_iota(jnp.int32, (chans, cols), 1)
    pair_out = out_ref[...]
    pbias = jnp.broadcast_to(pbias_ref[...], (chans, cols))

    def features(rounded, places):
        scaled = jnp.concatenate([pair_out * rounded[j:j + 1] for j in range(len(places))], axis=0)
        values = lax.dot_general(scaled.astype(BF16), factors, ROWS_BY_COLS, preferred_element_type=F32)
        for j, place in enumerate(places):
            for side, i in enumerate(place):
                value = values[j * chans:(j + 1) * chans, side * width:(side + 1) * width]
                own, beside = value[:, :cols] + pbias, value[:, cols:] + pbias
                if 0 <= i < rows:
                    feat[i // 2, :, (i % 2) * cols:(i % 2 + 1) * cols] = own
                zone = 6 if i < 0 else 8 if i >= rows else 4
                own = jnp.maximum(own, 0.0) * misc_ref[zone:zone + 1, :]
                beside = jnp.maximum(beside, 0.0) * misc_ref[zone + 1:zone + 2, :]
                before = pltpu.roll(jnp.where(lane >= cols - REACH, beside, own), REACH, 1)
                after = pltpu.roll(jnp.where(lane < REACH, beside, own), cols - REACH, 1)
                at = slice((i + REACH) * cols, (i + REACH + 1) * cols)
                hid[0:chans, at] = before.astype(BF16)
                hid[chans:2 * chans, at] = own.astype(BF16)
                hid[2 * chans:3 * chans, at] = after.astype(BF16)

    def rounded(x):
        return x.astype(BF16).astype(F32)

    features(rounded(misc_ref[REACH:2 * REACH, :]), [(rows + j, j - REACH) for j in range(REACH)])
    for m in range(0, half, GROUP):
        features(rounded(row_ref[m:m + GROUP, :]), [(m + j, half + m + j) for j in range(GROUP)])

    target_copy.wait()

    zero = jnp.zeros((chans, width), BF16)
    for tap, e in ((0, pairs - 2), (0, pairs - 1), (1, 0), (1, pairs - 1), (2, 0), (2, 1)):
        dif_taps[tap * chans:(tap + 1) * chans, e * width:(e + 1) * width] = zero
    cbias = jnp.broadcast_to(cbias_ref[...], (chans, width))
    keep = jnp.concatenate([misc_ref[4:5, :]] * 2, axis=1)
    bias_sum[...] = jnp.zeros_like(bias_sum)
    for e in range(pairs):
        part = jnp.dot(weight_ref[...], hid[:, e * width:(e + 1) * width], preferred_element_type=F32)
        m = e - 2
        if m >= 0:
            if (2 * m) % 16 == 0:
                targets = jnp.swapaxes(target_ref[:, 2 * m:2 * m + 16, :], 0, 1)
            at = (2 * m) % 16
            target = jnp.concatenate([targets[at], targets[at + 1]], axis=1).astype(F32)
            out = near[...] + part[2 * chans:]
            differ = keep * (feat[m] + (out + cbias) - target)
            loss = 0.5 * jnp.sum(differ * differ, axis=0, keepdims=True)
            loss_ref[2 * m:2 * m + 1, :] = loss[:, :cols]
            loss_ref[2 * m + 1:2 * m + 2, :] = loss[:, cols:]
            bias_sum[...] += differ
            grad_in = differ.astype(BF16)
            for tap in range(3):
                dif_taps[tap * chans:(tap + 1) * chans, (m + tap) * width:(m + tap + 1) * width] = grad_in
        if e > 0:
            near[...] = far[...] + part[chans:2 * chans]
        far[...] = part[0:chans]

    grad = lax.dot_general(hid[...], dif_taps[...], ROWS_BY_COLS, preferred_element_type=F32) * norm
    split = taps // 2
    grad_ref[0:taps, :] = grad[:, 0:2 * chans]
    last = grad[:, 2 * chans:]
    grad_ref[taps:taps + split, :] = jnp.concatenate([last[:split], last[split:]], axis=1)
    sums = bias_sum[:, :cols] + bias_sum[:, cols:]
    bias = lax.dot_general(
        jnp.ones((8, cols), F32), sums, ROWS_BY_COLS, preferred_element_type=F32, precision=lax.Precision.HIGHEST
    )
    grad_ref[taps + split:, :] = jnp.zeros((grad_ref.shape[0] - taps - split, 2 * chans), F32)
    grad_ref[taps + split:taps + split + 8, 0:chans] = bias * norm


GROUP = 2


def per_device(
    emb_row, emb_col, proj_row, proj_col, pair_out, pair_bias, conv_weight, conv_bias, target, kept_tiles
):
    chans, rows, cols = target.shape
    rank = pair_out.shape[0]
    row, col, rep = (lax.axis_index(axis) for axis in MESH)
    n_row, n_col, n_rep = (lax.axis_size(axis) for axis in MESH)
    edge = rows // kept_tiles.shape[0]
    half, wide = rows // 2, 2 * rank
    vmem = pl.BlockSpec(memory_space=pltpu.VMEM)

    shares = emb_row.shape[1], emb_col.shape[1]
    sliced = (shares[0] % 128 == 0, shares[1] % 16 == 0)
    projs = [proj_row.T, proj_col.T]
    for side, place in enumerate((col, row)):
        if not sliced[side]:
            projs[side] = lax.dynamic_slice_in_dim(projs[side], place * shares[side], shares[side], 1)
    zeros = pl.pallas_call(
        zeros_kernel,
        out_shape=jax.ShapeDtypeStruct((8, wide), F32),
        out_specs=vmem,
        compiler_params=pltpu.CompilerParams(vmem_limit_bytes=4 * 1024 * 1024),
        cost_estimate=pl.CostEstimate(flops=4 * 10**9, bytes_accessed=1000, transcendentals=0),
        name="zeros",
    )()
    col_send, row_send, cross_send = pl.pallas_call(
        functools.partial(project_kernel, sliced=sliced),
        out_shape=(
            jax.ShapeDtypeStruct((half + 8, wide), F32),
            jax.ShapeDtypeStruct((half + 8, wide), F32),
            jax.ShapeDtypeStruct((8, wide), F32),
        ),
        in_specs=[vmem] * 6,
        out_specs=(vmem,) * 3,
        scratch_shapes=[pltpu.VMEM((projs[1].shape[1], cols), BF16)],
        compiler_params=pltpu.CompilerParams(vmem_limit_bytes=4 * 1024 * 1024),
        cost_estimate=pl.CostEstimate(flops=2 * 10**9, bytes_accessed=1000, transcendentals=0),
        name="project",
    )(zeros, kept_tiles, emb_row, projs[0], emb_col.T, projs[1])

    shift = [[(i, (i + k) % n_col) for i in range(n_col)] for k in range(n_col)]
    row_cols = ("row", "col", "rep")

    def cross(x, k):
        def index(r, c, p):
            return (r * n_col + c) * n_rep + p

        return lax.ppermute(
            x, row_cols,
            [
                (index(r, c, p), index(r ^ 1, (c + k) % n_col, p ^ 1))
                for r in range(n_row) for c in range(n_col) for p in range(n_rep)
            ],
        )

    from_cross = {k: cross(cross_send, k) for k in range(1, n_col)}
    from_col = {k: lax.ppermute(col_send, "col", shift[k]) for k in range(1, n_col)}
    from_row = swap(row_send, row=1, rep=1)

    lane = lax.broadcasted_iota(jnp.int32, (1, wide), 1)
    lower = lane < rank

    def sides(blocks, at, size):
        return jnp.where(lower, blocks[n_col - 1][at:at + size], blocks[1][at:at + size])

    def outside(mask):
        return jnp.where(jnp.where(lower, col < n_col - 1, col > 0), mask, 0.0)

    row_sum = col_send[:half] + sum(from_col[k][:half] for k in from_col)
    col_sum = row_send[:half] + from_row[:half]
    side = sides(from_col, half, REACH) + sides(from_cross, REACH + 1, REACH)
    own_kept = col_send[half + REACH:half + REACH + 1]
    own_masks = jnp.concatenate([own_kept, outside(sides(from_col, half + REACH, 1))], axis=0)
    own_ends = jnp.where(lower, row_sum[:REACH], row_sum[half - REACH:])
    block = jnp.concatenate(
        [
            from_row[half:half + REACH] + sum(from_cross[k][:REACH] for k in from_cross),
            from_row[half + REACH:half + REACH + 1],
            outside(sides(from_cross, REACH, 1)),
        ],
        axis=0,
    )
    mate = swap(jnp.concatenate([own_ends, own_masks, jnp.zeros((4, wide), F32)], axis=0), rep=1)

    blocks = {1: block}
    pad = jnp.zeros((2, wide), F32)
    for step in steps("row", 2):
        got = swap(jnp.concatenate([col_sum, side, blocks[step - 1], pad], axis=0), row=step)
        col_sum = col_sum + got[:half]
        side = side + got[half:half + REACH]
        blocks[2 * step - 1] = got[half + REACH:half + REACH + 4]

    beyond = jnp.where(rep == 0, row - 1, row + 1)
    far = blocks[1]
    for apart, found in blocks.items():
        far = jnp.where((row ^ beyond) == apart, found, far)
    far_masks = jnp.where((beyond >= 0) & (beyond < n_row), far[REACH:], 0.0)
    above = jnp.where(rep == 0, far[:REACH], mate[:REACH])
    below = jnp.where(rep == 0, mate[:REACH], far[:REACH])
    mate_masks = mate[REACH:REACH + 2]
    misc = jnp.concatenate(
        [
            side,
            jnp.where(lower, below, above),
            own_masks,
            jnp.where(rep == 0, far_masks, mate_masks),
            jnp.where(rep == 0, mate_masks, far_masks),
            jnp.zeros((6, wide), F32),
        ],
        axis=0,
    )

    cells = (rows + 2 * REACH) * cols
    taps = 3 * chans
    weight = conv_weight.transpose(0, 3, 1, 2).reshape(taps, taps)
    packed = taps + taps // 2 + 16
    out_t = pair_out.astype(F32).T
    cell_loss, grads = pl.pallas_call(
        functools.partial(tile_kernel, norm=1.0 / (edge * edge)),
        out_shape=(
            jax.ShapeDtypeStruct((rows, cols), F32),
            jax.ShapeDtypeStruct((packed, 2 * chans), F32),
        ),
        in_specs=[vmem] * 7 + [pl.BlockSpec(memory_space=pltpu.HBM)],
        out_specs=(vmem,) * 2,
        scratch_shapes=[
            pltpu.VMEM(target.shape, BF16),
            pltpu.SemaphoreType.DMA,
            pltpu.VMEM((taps, cells), BF16),
            pltpu.VMEM((taps, cells), BF16),
            pltpu.VMEM((rows // 2, chans, 2 * cols), F32),
            pltpu.VMEM((4 * cols, wide), F32),
            pltpu.VMEM((chans, 2 * cols), F32),
            pltpu.VMEM((chans, 2 * cols), F32),
            pltpu.VMEM((chans, 2 * cols), F32),
        ],
        compiler_params=pltpu.CompilerParams(vmem_limit_bytes=40 * 1024 * 1024),
        name="tile",
    )(
        row_sum, col_sum, misc, jnp.concatenate([out_t, out_t], axis=1), pair_bias[:, None], weight,
        conv_bias[:, None], target,
    )

    piece = packed // n_rep
    mine = lax.dynamic_slice_in_dim(grads, rep * piece, piece, 0)
    total = mine + swap(lax.dynamic_slice_in_dim(grads, (1 - rep) * piece, piece, 0), rep=1)
    corner = swap(total, row=1, col=1)
    beside = swap(total, col=1)
    total = (total + beside) + (swap(total, row=1) + corner)
    for step in steps("col", 2):
        total = total + swap(total, col=step)
    for step in steps("row", 2):
        total = total + swap(total, row=step)
    other = swap(total, rep=1)
    grads = jnp.concatenate([jnp.where(rep == 0, total, other), jnp.where(rep == 0, other, total)], axis=0)
    main = grads[:taps].reshape(3, chans, 2, chans).transpose(2, 0, 1, 3)
    last = grads[taps:taps + taps // 2]
    last = jnp.concatenate([last[:, :chans], last[:, chans:]], axis=0).reshape(1, 3, chans, chans)
    grad_conv = jnp.concatenate([main, last], axis=0)
    grad_bias = grads[taps + taps // 2, :chans]
    return cell_loss, grad_conv, grad_bias


def solution(mesh):
    in_specs = (
        P(("grp", "row", "rep"), "col"),
        P(("grp", "col"), "row"),
        P(),
        P(),
        P(),
        P(),
        P(),
        P(),
        P(None, ("grp", "row", "rep"), "col"),
        P(("grp", "row", "rep"), "col"),
    )
    out_specs = (P(("grp", "row", "rep"), "col"), P("grp", None, None, None), P("grp"))
    return jax.shard_map(
        per_device, mesh=mesh, in_specs=in_specs, out_specs=out_specs, check_vma=False
    )
```

profile of v0, /device:TPU:0, one launch (start us, length us, event | category | flops | bytes accessed | tf_op | source)
XLA Modules:
  0.0 40.7 jit_solution(18051045234125474228)
XLA Ops:
  1.4 0.2 copy-done.3
  1.8 0.4 %project.1 = (f32[72,128]{1,0:T(8,128)S(1)}, f32[72,128]{1,0:T(8,128)S(1)}, f32[8,128]{1,0:T(8,128)S(1)}) custom-call(f32[8,128]{1,0:T(8,128)S(1)} %zeros.1.zeros_ref, s32[1,1]{1,0:T(1,128)S(6)} %copy.25.kept_ref, bf16[128,640]{1,0:T(8,128)(2,1)S(1)} %copy-done.1, bf16[64,1280]{1,0:T(8,128)(2,1)S(1)} %bitcast.13, bf16[320,128]{1,0:T(8,128)(2,1)S(1)} %bitcast.15, ...), custom_call_target="tpu_custom_call" | custom-call | flops 2000000000 | bytes 1000 | tf_op jit(solution)/shard_map/project/pallas_call | solution.py:205
  2.2 3.5 %collective-permute-start.2 = (f32[8,128]{1,0:T(8,128)S(1)}, f32[8,128]{1,0:T(8,128)S(1)}, u32[]{:S(2)}, u32[]{:S(2)}) collective-permute-start(f32[8,128]{1,0:T(8,128)S(1)} %get-tuple-element.10), channel_id=1, source_target_pairs={{0,7},{1,6},{2,5},{3,4},{4,3},{5,2},{6,1},{7,0},{8,15},{9,14},{10,... | collective-permute-start | bytes 12296 | tf_op jit(solution)/shard_map/ppermute | solution.py:227
  5.7 0.7 %collective-permute-start.1 = (f32[72,128]{1,0:T(8,128)S(1)}, f32[72,128]{1,0:T(8,128)S(1)}, u32[]{:S(2)}, u32[]{:S(2)}) collective-permute-start(f32[72,128]{1,0:T(8,128)S(1)} %get-tuple-element.9), channel_id=1, source_target_pairs={{0,5},{1,4},{2,7},{3,6},{4,1},{5,0},{6,3},{7,2},{8,13},{9,12},{10,... | collective-permute-start | bytes 110600 | tf_op jit(solution)/shard_map/ppermute | solution.py:24
  6.8 0.2 copy.19
  7.0 0.2 reshape.28.weight_ref
  7.3 1.8 %collective-permute-done.1 = f32[72,128]{1,0:T(8,128)S(1)} collective-permute-done((f32[72,128]{1,0:T(8,128)S(1)}, f32[72,128]{1,0:T(8,128)S(1)}, u32[]{:S(2)}, u32[]{:S(2)}) %collective-permute-start.1) | collective-permute-done | bytes 36896 | tf_op jit(solution)/shard_map/ppermute | solution.py:24
  9.1 1.3 %collective-permute-done = f32[72,128]{1,0:T(8,128)S(1)} collective-permute-done((f32[72,128]{1,0:T(8,128)S(1)}, f32[72,128]{1,0:T(8,128)S(1)}, u32[]{:S(2)}, u32[]{:S(2)}) %collective-permute-start) | collective-permute-done | bytes 36896 | tf_op jit(solution)/shard_map/ppermute | solution.py:236
  10.4 2.7 %collective-permute-start.3 = (f32[72,128]{1,0:T(8,128)S(1)}, f32[72,128]{1,0:T(8,128)S(1)}, u32[]{:S(2)}, u32[]{:S(2)}) collective-permute-start(f32[72,128]{1,0:T(8,128)S(1)} %concatenate.30), channel_id=1, source_target_pairs={{0,8},{1,9},{2,10},{3,11},{4,12},{5,13},{6,14},{7,15},{8,0},{9,1},... | collective-permute-start | bytes 110600 | tf_op jit(solution)/shard_map/ppermute | solution.py:24
  13.2 2.1 %collective-permute-done.3 = f32[72,128]{1,0:T(8,128)S(1)} collective-permute-done((f32[72,128]{1,0:T(8,128)S(1)}, f32[72,128]{1,0:T(8,128)S(1)}, u32[]{:S(2)}, u32[]{:S(2)}) %collective-permute-start.3) | collective-permute-done | bytes 36896 | tf_op jit(solution)/shard_map/ppermute | solution.py:24
  15.4 7.0 %tile.1 = (f32[128,128]{1,0:T(8,128)}, f32[304,128]{1,0:T(8,128)S(1)}) custom-call(f32[64,128]{1,0:T(8,128)S(1)} %slice_add_fusion.2.row_ref, f32[64,128]{1,0:T(8,128)S(1)} %slice_add_fusion.col_ref, f32[16,128]{1,0:T(8,128)S(1)} %concatenate.33.misc_ref, f32[64,128]{1,0:T(8,128)S(1)} %maximum_convert_fusion.out_ref, f32[64,1]{1,0:T(8,128)S(1)} %copy.20.pbias_ref, ...), custom_call_target="tpu_custom_call" | custom-call | tf_op jit(solution)/shard_map/tile/pallas_call | solution.py:297
  22.6 1.3 %collective-permute-done.5 = f32[152,128]{1,0:T(8,128)S(1)} collective-permute-done((f32[152,128]{1,0:T(8,128)S(1)}, f32[152,128]{1,0:T(8,128)S(1)}, u32[]{:S(2)}, u32[]{:S(2)}) %collective-permute-start.5) | collective-permute-done | bytes 77856 | tf_op jit(solution)/shard_map/ppermute | solution.py:24
  23.8 1.6 %collective-permute-start.8 = (f32[152,128]{1,0:T(8,128)S(1)}, f32[152,128]{1,0:T(8,128)S(1)}, u32[]{:S(2)}, u32[]{:S(2)}) collective-permute-start(f32[152,128]{1,0:T(8,128)S(1)} %dynamic-slice_add_fusion), channel_id=1, source_target_pairs={{0,6},{1,7},{2,4},{3,5},{4,2},{5,3},{6,0},{7,1},{8,14},{9,15},{10,... | collective-permute-start | bytes 233480 | tf_op jit(solution)/shard_map/ppermute | solution.py:24
  25.4 0.1 collective-permute-start.7
  25.6 1.8 %collective-permute-start.6 = (f32[152,128]{1,0:T(8,128)S(1)}, f32[152,128]{1,0:T(8,128)S(1)}, u32[]{:S(2)}, u32[]{:S(2)}) collective-permute-start(f32[152,128]{1,0:T(8,128)S(1)} %dynamic-slice_add_fusion), channel_id=1, source_target_pairs={{0,2},{1,3},{2,0},{3,1},{4,6},{5,7},{6,4},{7,5},{8,10},{9,11},{10,... | collective-permute-start | bytes 233480 | tf_op jit(solution)/shard_map/ppermute | solution.py:24
  27.4 2.3 %collective-permute-done.8 = f32[152,128]{1,0:T(8,128)S(1)} collective-permute-done((f32[152,128]{1,0:T(8,128)S(1)}, f32[152,128]{1,0:T(8,128)S(1)}, u32[]{:S(2)}, u32[]{:S(2)}) %collective-permute-start.8) | collective-permute-done | bytes 77856 | tf_op jit(solution)/shard_map/ppermute | solution.py:24
  29.7 0.2 collective-permute-done.7
  29.8 1.0 %collective-permute-done.6 = f32[152,128]{1,0:T(8,128)S(1)} collective-permute-done((f32[152,128]{1,0:T(8,128)S(1)}, f32[152,128]{1,0:T(8,128)S(1)}, u32[]{:S(2)}, u32[]{:S(2)}) %collective-permute-start.6) | collective-permute-done | bytes 77856 | tf_op jit(solution)/shard_map/ppermute | solution.py:24
  30.9 2.7 %collective-permute-start.9 = (f32[152,128]{1,0:T(8,128)S(1)}, f32[152,128]{1,0:T(8,128)S(1)}, u32[]{:S(2)}, u32[]{:S(2)}) collective-permute-start(f32[152,128]{1,0:T(8,128)S(1)} %add_add_fusion), channel_id=1, source_target_pairs={{0,8},{1,9},{2,10},{3,11},{4,12},{5,13},{6,14},{7,15},{8,0},{9,1},... | collective-permute-start | bytes 233480 | tf_op jit(solution)/shard_map/ppermute | solution.py:24
  33.6 4.2 %collective-permute-done.9 = f32[152,128]{1,0:T(8,128)S(1)} collective-permute-done((f32[152,128]{1,0:T(8,128)S(1)}, f32[152,128]{1,0:T(8,128)S(1)}, u32[]{:S(2)}, u32[]{:S(2)}) %collective-permute-start.9) | collective-permute-done | bytes 77856 | tf_op jit(solution)/shard_map/ppermute | solution.py:24
  37.9 1.3 %collective-permute-done.10 = f32[152,128]{1,0:T(8,128)S(1)} collective-permute-done((f32[152,128]{1,0:T(8,128)S(1)}, f32[152,128]{1,0:T(8,128)S(1)}, u32[]{:S(2)}, u32[]{:S(2)}) %collective-permute-start.10) | collective-permute-done | bytes 77856 | tf_op jit(solution)/shard_map/ppermute | solution.py:24
  39.1 0.5 %slice_bitcast_fusion = f32[64]{0:T(128)} fusion(f32[152,128]{1,0:T(8,128)S(1)} %get-tuple-element.14), kind=kLoop, calls=%fused_computation.23 | loop fusion | bytes 512 | tf_op jit(solution)/shard_map/squeeze | solution.py:339
  39.7 0.2 reshape.29
  39.9 0.7 %pad_maximum_fusion = f32[3,3,64,64]{3,2,1,0:T(8,128)} fusion(f32[1,3,64,64]{3,2,1,0:T(8,128)S(1)} %bitcast.17, f32[2,3,64,64]{3,2,1,0:T(8,128)S(1)} %bitcast.16), kind=kLoop, calls=%fused_computation | loop fusion | flops 36864 | bytes 294912 | tf_op jit(solution)/shard_map/concatenate | solution.py:338
  (57 shorter events, 1.3 us)
Async XLA Ops:
  0.6 0.9 %copy-start.3 = (bf16[1280,64]{0,1:T(8,128)(2,1)S(1)}, bf16[1280,64]{0,1:T(8,128)(2,1)}, u32[]{:S(2)}) copy-start(bf16[1280,64]{0,1:T(8,128)(2,1)} %param.13) | copy-start | bytes 491524
  0.6 1.0 %copy-start.2 = (bf16[1280,64]{0,1:T(8,128)(2,1)S(1)}, bf16[1280,64]{0,1:T(8,128)(2,1)}, u32[]{:S(2)}) copy-start(bf16[1280,64]{0,1:T(8,128)(2,1)} %param.12) | copy-start | bytes 491524
  0.7 1.0 %copy-start.4 = (bf16[128,320]{0,1:T(8,128)(2,1)S(1)}, bf16[128,320]{0,1:T(8,128)(2,1)}, u32[]{:S(2)}) copy-start(bf16[128,320]{0,1:T(8,128)(2,1)} %param.11) | copy-start | bytes 245764
  0.7 1.1 %copy-start.1 = (bf16[128,640]{1,0:T(8,128)(2,1)S(1)}, bf16[128,640]{1,0:T(8,128)(2,1)}, u32[]{:S(2)}) copy-start(bf16[128,640]{1,0:T(8,128)(2,1)} %row_ref.1) | copy-start | bytes 491524
  1.8 4.6 %copy-start.6 = (bf16[64,64]{1,0:T(8,128)(2,1)S(1)}, bf16[64,64]{1,0:T(8,128)(2,1)}, u32[]{:S(2)}) copy-start(bf16[64,64]{1,0:T(8,128)(2,1)} %param.14) | copy-start | bytes 24580
  1.8 4.9 %copy-start.7 = (f32[64]{0:T(128)S(1)}, f32[64]{0:T(128)}, u32[]{:S(2)}) copy-start(f32[64]{0:T(128)} %param.15) | copy-start | bytes 772
  1.8 5.0 %copy-start.8 = (f32[64]{0:T(128)S(1)}, f32[64]{0:T(128)}, u32[]{:S(2)}) copy-start(f32[64]{0:T(128)} %param.17) | copy-start | bytes 772
  1.8 5.1 %copy-start.5 = (bf16[3,3,64,64]{3,2,1,0:T(8,128)(2,1)S(1)}, bf16[3,3,64,64]{3,2,1,0:T(8,128)(2,1)}, u32[]{:S(2)}) copy-start(bf16[3,3,64,64]{3,2,1,0:T(8,128)(2,1)} %param.16) | copy-start | bytes 221188
  1.8 13.6 %copy-start = (bf16[64,128,128]{2,1,0:T(8,128)(2,1)S(1)}, bf16[64,128,128]{2,1,0:T(8,128)(2,1)}, u32[]{:S(2)}) copy-start(bf16[64,128,128]{2,1,0:T(8,128)(2,1)} %target_hbm.1) | copy-start | bytes 6291460
  2.2 5.0 %collective-permute-start.2 = (f32[8,128]{1,0:T(8,128)S(1)}, f32[8,128]{1,0:T(8,128)S(1)}, u32[]{:S(2)}, u32[]{:S(2)}) collective-permute-start(f32[8,128]{1,0:T(8,128)S(1)} %get-tuple-element.10), channel_id=1, source_target_pairs={{0,7},{1,6},{2,5},{3,4},{4,3},{5,2},{6,1},{7,0},{8,15},{9,14},{10,... | collective-permute-start | bytes 12296 | tf_op jit(solution)/shard_map/ppermute | solution.py:227
  5.7 3.4 %collective-permute-start.1 = (f32[72,128]{1,0:T(8,128)S(1)}, f32[72,128]{1,0:T(8,128)S(1)}, u32[]{:S(2)}, u32[]{:S(2)}) collective-permute-start(f32[72,128]{1,0:T(8,128)S(1)} %get-tuple-element.9), channel_id=1, source_target_pairs={{0,5},{1,4},{2,7},{3,6},{4,1},{5,0},{6,3},{7,2},{8,13},{9,12},{10,... | collective-permute-start | bytes 110600 | tf_op jit(solution)/shard_map/ppermute | solution.py:24
  6.4 4.0 %collective-permute-start = (f32[72,128]{1,0:T(8,128)S(1)}, f32[72,128]{1,0:T(8,128)S(1)}, u32[]{:S(2)}, u32[]{:S(2)}) collective-permute-start(f32[72,128]{1,0:T(8,128)S(1)} %get-tuple-element.8), channel_id=1, source_target_pairs={{0,2},{2,0},{1,3},{3,1},{4,6},{6,4},{5,7},{7,5},{8,10},{10,8},{9,1... | collective-permute-start | bytes 110600 | tf_op jit(solution)/shard_map/ppermute | solution.py:236
  10.4 4.9 %collective-permute-start.3 = (f32[72,128]{1,0:T(8,128)S(1)}, f32[72,128]{1,0:T(8,128)S(1)}, u32[]{:S(2)}, u32[]{:S(2)}) collective-permute-start(f32[72,128]{1,0:T(8,128)S(1)} %concatenate.30), channel_id=1, source_target_pairs={{0,8},{1,9},{2,10},{3,11},{4,12},{5,13},{6,14},{7,15},{8,0},{9,1},... | collective-permute-start | bytes 110600 | tf_op jit(solution)/shard_map/ppermute | solution.py:24
  13.2 2.2 %collective-permute-start.4 = (f32[8,128]{1,0:T(8,128)S(1)}, f32[8,128]{1,0:T(8,128)S(1)}, u32[]{:S(2)}, u32[]{:S(2)}) collective-permute-start(f32[8,128]{1,0:T(8,128)S(1)} %maximum_maximum_fusion), channel_id=1, source_target_pairs={{0,1},{1,0},{2,3},{3,2},{4,5},{5,4},{6,7},{7,6},{8,9},{9,8},{10,11... | collective-permute-start | bytes 12296 | tf_op jit(solution)/shard_map/ppermute | solution.py:24
  22.5 1.3 %collective-permute-start.5 = (f32[152,128]{1,0:T(8,128)S(1)}, f32[152,128]{1,0:T(8,128)S(1)}, u32[]{:S(2)}, u32[]{:S(2)}) collective-permute-start(f32[152,128]{1,0:T(8,128)S(1)} %constant_dynamic-slice_fusion), channel_id=1, source_target_pairs={{0,1},{1,0},{2,3},{3,2},{4,5},{5,4},{6,7},{7,6},{8,9},{9,8},{10,11... | collective-permute-start | bytes 233480 | tf_op jit(solution)/shard_map/ppermute | solution.py:24
  23.8 5.8 %collective-permute-start.8 = (f32[152,128]{1,0:T(8,128)S(1)}, f32[152,128]{1,0:T(8,128)S(1)}, u32[]{:S(2)}, u32[]{:S(2)}) collective-permute-start(f32[152,128]{1,0:T(8,128)S(1)} %dynamic-slice_add_fusion), channel_id=1, source_target_pairs={{0,6},{1,7},{2,4},{3,5},{4,2},{5,3},{6,0},{7,1},{8,14},{9,15},{10,... | collective-permute-start | bytes 233480 | tf_op jit(solution)/shard_map/ppermute | solution.py:24
  25.4 4.4 %collective-permute-start.7 = (f32[152,128]{1,0:T(8,128)S(1)}, f32[152,128]{1,0:T(8,128)S(1)}, u32[]{:S(2)}, u32[]{:S(2)}) collective-permute-start(f32[152,128]{1,0:T(8,128)S(1)} %dynamic-slice_add_fusion), channel_id=1, source_target_pairs={{0,4},{1,5},{2,6},{3,7},{4,0},{5,1},{6,2},{7,3},{8,12},{9,13},{10,... | collective-permute-start | bytes 233480 | tf_op jit(solution)/shard_map/ppermute | solution.py:24
  25.6 5.3 %collective-permute-start.6 = (f32[152,128]{1,0:T(8,128)S(1)}, f32[152,128]{1,0:T(8,128)S(1)}, u32[]{:S(2)}, u32[]{:S(2)}) collective-permute-start(f32[152,128]{1,0:T(8,128)S(1)} %dynamic-slice_add_fusion), channel_id=1, source_target_pairs={{0,2},{1,3},{2,0},{3,1},{4,6},{5,7},{6,4},{7,5},{8,10},{9,11},{10,... | collective-permute-start | bytes 233480 | tf_op jit(solution)/shard_map/ppermute | solution.py:24
  30.9 6.9 %collective-permute-start.9 = (f32[152,128]{1,0:T(8,128)S(1)}, f32[152,128]{1,0:T(8,128)S(1)}, u32[]{:S(2)}, u32[]{:S(2)}) collective-permute-start(f32[152,128]{1,0:T(8,128)S(1)} %add_add_fusion), channel_id=1, source_target_pairs={{0,8},{1,9},{2,10},{3,11},{4,12},{5,13},{6,14},{7,15},{8,0},{9,1},... | collective-permute-start | bytes 233480 | tf_op jit(solution)/shard_map/ppermute | solution.py:24
  37.8 1.3 %collective-permute-start.10 = (f32[152,128]{1,0:T(8,128)S(1)}, f32[152,128]{1,0:T(8,128)S(1)}, u32[]{:S(2)}, u32[]{:S(2)}) collective-permute-start(f32[152,128]{1,0:T(8,128)S(1)} %add.56), channel_id=1, source_target_pairs={{0,1},{1,0},{2,3},{3,2},{4,5},{5,4},{6,7},{7,6},{8,9},{9,8},{10,11... | collective-permute-start | bytes 233480 | tf_op jit(solution)/shard_map/ppermute | solution.py:24
where the time goes:
time: 40.8 us; the launch traced here: 40.7 us
  waiting for transfers between devices  15.4 us (38%)
  starting transfers between devices  13.2 us (32%)
  Pallas kernels  7.44 us (18%)
  local copies, waits for them, and re-layouts  1.96 us (5%)
  between operations  1.6 us (4%)
  other arithmetic  1.04 us (3%)
    ppermute x9, waiting for transfers between devices, swap(): lax.ppermute(x, MESH, [(index(r, c, p), index(r ^ row, c ^ col, p ^ rep))...  14.1 us
    ppermute x9, starting transfers between devices, swap(): lax.ppermute(x, MESH, [(index(r, c, p), index(r ^ row, c ^ col, p ^ rep))...  9.78 us
    pallas_call x1, Pallas kernels, per_device(): pl.pallas_call(functools.partial(tile_kernel, norm=1.0 / (edge * edge)),...  7.02 us
    ppermute x1, starting transfers between devices, cross(): lax.ppermute(x, row_cols, [(index(r, c, p), index(r ^ 1, (c + k) % n_col,...  3.46 us
    ppermute x1, waiting for transfers between devices, per_device(): lax.ppermute(col_send, 'col', shift[k])  1.29 us
  transfers between devices with their start and end apart: 11, of which 9 were waited for; matrix products, arithmetic and copies ran while one was open for 2% of the time, Pallas kernels for 0%

commit v1 on v0

--- a/solution.py
+++ b/solution.py
@@ -75,8 +75,8 @@
 
 
 def tile_kernel(
-    row_ref, col_ref, misc_ref, out_ref, pbias_ref, weight_ref, cbias_ref, target_hbm,
-    loss_ref, grad_ref, target_ref, sem, hid, dif_taps, feat, rhs, near, far, bias_sum, *, norm
+    row_ref, col_ref, misc_ref, out_ref, pbias_ref, weight_ref, cbias_ref, target_ref,
+    loss_ref, grad_ref, hid, dif_taps, feat, rhs, turned_target, *, norm
 ):
     chans, rows, cols = target_ref.shape
     half, wide = row_ref.shape
@@ -85,41 +85,56 @@
     pairs = rows // 2 + 2
     taps = weight_ref.shape[0]
 
-    target_copy = pltpu.make_async_copy(target_hbm, target_ref, sem)
-    target_copy.start()
-
+    kept = misc_ref[4:5, 0:1]
+    lane = lax.broadcasted_iota(jnp.int32, (half, wide), 1)
     rhs[...] = jnp.zeros_like(rhs)
-    lane = lax.broadcasted_iota(jnp.int32, (half, wide), 1)
-    for start, value in ((0, col_ref[...]), (cols, misc_ref[0:REACH, :])):
+    after_map, before_map = misc_ref[5:6, 0:1], misc_ref[5:6, wide - 1:wide]
+    one = jnp.ones((1, 1), F32)
+    pieces = ((0, col_ref[...], half, kept, kept), (cols, misc_ref[0:REACH, :], cols - REACH, after_map, before_map))
+    for start, value, gap, mask_first, mask_last in pieces:
         turned = pltpu.roll(value, rank, 1)
         size = value.shape[0]
         lower = lane[:size] < rank
-        gap = half if start == 0 else cols - REACH
         for base, first, last in ((0, value, turned), (2 * cols, turned, value)):
             keep_half = lower if base == 0 else ~lower
             at = base + start
-            rhs[at:at + size, :] = jnp.where(keep_half, first, 0.0)
-            rhs[at + gap:at + gap + size, :] = jnp.where(keep_half, last, 0.0)
-    factors = rhs[...].astype(BF16)
+            for x, mask in ((first, mask_first), (last, mask_last)):
+                x = jnp.where(keep_half, x, 0.0)
+                for plane, factor in enumerate((mask, one)):
+                    rhs[plane, at:at + size, :wide] = x * factor
+                    rhs[plane, at:at + size, wide:] = jnp.where(lane[:size] < 3, factor, 0.0)
+                at += gap
+    factors = [rhs[plane].astype(BF16) for plane in range(2)]
 
     lane = lax.broadcasted_iota(jnp.int32, (chans, cols), 1)
     pair_out = out_ref[...]
-    pbias = jnp.broadcast_to(pbias_ref[...], (chans, cols))
-
-    def features(rounded, places):
+    high = pbias_ref[...].astype(BF16).astype(F32)
+    rest = pbias_ref[...] - high
+    middle = rest.astype(BF16).astype(F32)
+    bias_parts = jnp.where(
+        lane == 0, high, jnp.where(lane == 1, middle, jnp.where(lane == 2, rest - middle, 0.0))
+    ).astype(BF16)
+    last_two, first_two = lane >= cols - REACH, lane < REACH
+
+    def features(rounded, places, plane):
         scaled = jnp.concatenate([pair_out * rounded[j:j + 1] for j in range(len(places))], axis=0)
-        values = lax.dot_general(scaled.astype(BF16), factors, ROWS_BY_COLS, preferred_element_type=F32)
+        scaled = jnp.concatenate(
+            [scaled.astype(BF16), jnp.concatenate([bias_parts] * len(places), axis=0)], axis=1
+        )
+        values = lax.dot_general(scaled, factors[plane], ROWS_BY_COLS, preferred_element_type=F32)
         for j, place in enumerate(places):
             for side, i in enumerate(place):
                 value = values[j * chans:(j + 1) * chans, side * width:(side + 1) * width]
-                own, beside = value[:, :cols] + pbias, value[:, cols:] + pbias
-                if 0 <= i < rows:
+                own, beside = value[:, :cols], value[:, cols:]
+                if plane == 0:
                     feat[i // 2, :, (i % 2) * cols:(i % 2 + 1) * cols] = own
-                zone = 6 if i < 0 else 8 if i >= rows else 4
-                own = jnp.maximum(own, 0.0) * misc_ref[zone:zone + 1, :]
-                beside = jnp.maximum(beside, 0.0) * misc_ref[zone + 1:zone + 2, :]
-                before = pltpu.roll(jnp.where(lane >= cols - REACH, beside, own), REACH, 1)
-                after = pltpu.roll(jnp.where(lane < REACH, beside, own), cols - REACH, 1)
+                else:
+                    zone = 6 if i < 0 else 8
+                    own = own * misc_ref[zone:zone + 1, :]
+                    beside = beside * misc_ref[zone + 1:zone + 2, :]
+                own, beside = (jnp.maximum(x.astype(BF16), 0) for x in (own, beside))
+                before = pltpu.roll(jnp.where(last_two, beside, own), REACH, 1)
+                after = pltpu.roll(jnp.where(first_two, beside, own), cols - REACH, 1)
                 at = slice((i + REACH) * cols, (i + REACH + 1) * cols)
                 hid[0:chans, at] = before.astype(BF16)
                 hid[chans:2 * chans, at] = own.astype(BF16)
@@ -128,38 +143,35 @@
     def rounded(x):
         return x.astype(BF16).astype(F32)
 
-    features(rounded(misc_ref[REACH:2 * REACH, :]), [(rows + j, j - REACH) for j in range(REACH)])
+    features(rounded(misc_ref[REACH:2 * REACH, :]), [(rows + j, j - REACH) for j in range(REACH)], 1)
     for m in range(0, half, GROUP):
-        features(rounded(row_ref[m:m + GROUP, :]), [(m + j, half + m + j) for j in range(GROUP)])
-
-    target_copy.wait()
+        features(rounded(row_ref[m:m + GROUP, :]), [(m + j, half + m + j) for j in range(GROUP)], 0)
+        if (2 * m) % 16 == 0:
+            turned_target[2 * m:2 * m + 16] = jnp.swapaxes(target_ref[:, 2 * m:2 * m + 16, :], 0, 1)
 
     zero = jnp.zeros((chans, width), BF16)
     for tap, e in ((0, pairs - 2), (0, pairs - 1), (1, 0), (1, pairs - 1), (2, 0), (2, 1)):
         dif_taps[tap * chans:(tap + 1) * chans, e * width:(e + 1) * width] = zero
     cbias = jnp.broadcast_to(cbias_ref[...], (chans, width))
     keep = jnp.concatenate([misc_ref[4:5, :]] * 2, axis=1)
-    bias_sum[...] = jnp.zeros_like(bias_sum)
+    bias_sum = jnp.zeros((chans, width), F32)
     for e in range(pairs):
         part = jnp.dot(weight_ref[...], hid[:, e * width:(e + 1) * width], preferred_element_type=F32)
         m = e - 2
         if m >= 0:
-            if (2 * m) % 16 == 0:
-                targets = jnp.swapaxes(target_ref[:, 2 * m:2 * m + 16, :], 0, 1)
-            at = (2 * m) % 16
-            target = jnp.concatenate([targets[at], targets[at + 1]], axis=1).astype(F32)
-            out = near[...] + part[2 * chans:]
+            target = jnp.concatenate([turned_target[2 * m], turned_target[2 * m + 1]], axis=1).astype(F32)
+            out = near + part[2 * chans:]
             differ = keep * (feat[m] + (out + cbias) - target)
             loss = 0.5 * jnp.sum(differ * differ, axis=0, keepdims=True)
             loss_ref[2 * m:2 * m + 1, :] = loss[:, :cols]
             loss_ref[2 * m + 1:2 * m + 2, :] = loss[:, cols:]
-            bias_sum[...] += differ
+            bias_sum = bias_sum + differ
             grad_in = differ.astype(BF16)
             for tap in range(3):
                 dif_taps[tap * chans:(tap + 1) * chans, (m + tap) * width:(m + tap + 1) * width] = grad_in
         if e > 0:
-            near[...] = far[...] + part[chans:2 * chans]
-        far[...] = part[0:chans]
+            near = far + part[chans:2 * chans]
+        far = part[0:chans]
 
     grad = lax.dot_general(hid[...], dif_taps[...], ROWS_BY_COLS, preferred_element_type=F32) * norm
     split = taps // 2
@@ -174,7 +186,22 @@
     grad_ref[taps + split:taps + split + 8, 0:chans] = bias * norm
 
 
-GROUP = 2
+def unpack_kernel(own_ref, other_ref, conv_ref, bias_ref):
+    chans = conv_ref.shape[3]
+    first = lax.axis_index("rep") == 0
+    own, other = own_ref[...], other_ref[...]
+    whole = jnp.concatenate([jnp.where(first, own, other), jnp.where(first, other, own)], axis=0)
+    taps, split = 3 * chans, 3 * chans // 2
+    for a in range(2):
+        for b in range(3):
+            conv_ref[a, b] = whole[b * chans:(b + 1) * chans, a * chans:(a + 1) * chans]
+    last = jnp.concatenate([whole[taps:taps + split, :chans], whole[taps:taps + split, chans:]], axis=0)
+    for b in range(3):
+        conv_ref[2, b] = last[b * chans:(b + 1) * chans]
+    bias_ref[...] = whole[taps + split:taps + split + 1, :chans]
+
+
+GROUP = 4
 
 
 def per_device(
@@ -300,18 +327,14 @@
             jax.ShapeDtypeStruct((rows, cols), F32),
             jax.ShapeDtypeStruct((packed, 2 * chans), F32),
         ),
-        in_specs=[vmem] * 7 + [pl.BlockSpec(memory_space=pltpu.HBM)],
+        in_specs=[vmem] * 8,
         out_specs=(vmem,) * 2,
         scratch_shapes=[
-            pltpu.VMEM(target.shape, BF16),
-            pltpu.SemaphoreType.DMA,
             pltpu.VMEM((taps, cells), BF16),
             pltpu.VMEM((taps, cells), BF16),
             pltpu.VMEM((rows // 2, chans, 2 * cols), F32),
-            pltpu.VMEM((4 * cols, wide), F32),
-            pltpu.VMEM((chans, 2 * cols), F32),
-            pltpu.VMEM((chans, 2 * cols), F32),
-            pltpu.VMEM((chans, 2 * cols), F32),
+            pltpu.VMEM((2, 4 * cols, 2 * wide), F32),
+            pltpu.VMEM((rows, chans, cols), BF16),
         ],
         compiler_params=pltpu.CompilerParams(vmem_limit_bytes=40 * 1024 * 1024),
         name="tile",
@@ -331,13 +354,15 @@
     for step in steps("row", 2):
         total = total + swap(total, row=step)
     other = swap(total, rep=1)
-    grads = jnp.concatenate([jnp.where(rep == 0, total, other), jnp.where(rep == 0, other, total)], axis=0)
-    main = grads[:taps].reshape(3, chans, 2, chans).transpose(2, 0, 1, 3)
-    last = grads[taps:taps + taps // 2]
-    last = jnp.concatenate([last[:, :chans], last[:, chans:]], axis=0).reshape(1, 3, chans, chans)
-    grad_conv = jnp.concatenate([main, last], axis=0)
-    grad_bias = grads[taps + taps // 2, :chans]
-    return cell_loss, grad_conv, grad_bias
+    grad_conv, grad_bias = pl.pallas_call(
+        unpack_kernel,
+        out_shape=(jax.ShapeDtypeStruct((3, 3, chans, chans), F32), jax.ShapeDtypeStruct((1, chans), F32)),
+        in_specs=[vmem] * 2,
+        out_specs=(vmem,) * 2,
+        compiler_params=pltpu.CompilerParams(vmem_limit_bytes=4 * 1024 * 1024),
+        name="unpack",
+    )(total, other)
+    return cell_loss, grad_conv, grad_bias[0]
 
 
 def solution(mesh):

time: 40.8 us -> 38.7 us (0.949)
  other arithmetic: 1.04 us -> 0.26 us
  local copies, waits for them, and re-layouts: 1.96 us -> 1.19 us
  Pallas kernels: 7.44 us -> 6.95 us
    pallas_call x1, Pallas kernels: 7.02 us -> 5.69 us  [per_device(): pl.pallas_call(functools.partial(tile_kernel, norm=1.0 / (edge * edge)),...]
    pallas_call x0 -> x1, Pallas kernels: none -> 0.83 us  [per_device(): pl.pallas_call(unpack_kernel, out_shape=(jax.ShapeDtypeStruct((3, 3, chan...]
    concatenate x3 -> x0, other arithmetic: 0.76 us -> none  [the longest x1 0.74 us: per_device(): grad_conv = jnp.concatenate([main, last], axis=0)]
    squeeze x1 -> x0, local copies, waits for them, and re-layouts: 0.51 us -> none  [per_device(): grad_bias = grads[taps + taps // 2, :chans]]
where the time goes in v1:
time: 38.7 us; the launch traced here: 38.5 us
  waiting for transfers between devices  15.4 us (40%)
  starting transfers between devices  13.2 us (34%)
  Pallas kernels  6.95 us (18%)
  between operations  1.55 us (4%)
  local copies, waits for them, and re-layouts  1.19 us (3%)
    ppermute x9, waiting for transfers between devices, swap(): lax.ppermute(x, MESH, [(index(r, c, p), index(r ^ row, c ^ col, p ^ rep))...  14.1 us
    ppermute x9, starting transfers between devices, swap(): lax.ppermute(x, MESH, [(index(r, c, p), index(r ^ row, c ^ col, p ^ rep))...  9.72 us
    pallas_call x1, Pallas kernels, per_device(): pl.pallas_call(functools.partial(tile_kernel, norm=1.0 / (edge * edge)),...  5.69 us
    ppermute x1, starting transfers between devices, cross(): lax.ppermute(x, row_cols, [(index(r, c, p), index(r ^ 1, (c + k) % n_col,...  3.46 us
    ppermute x1, waiting for transfers between devices, per_device(): lax.ppermute(col_send, 'col', shift[k])  1.29 us
    pallas_call x1, Pallas kernels, per_device(): pl.pallas_call(unpack_kernel, out_shape=(jax.ShapeDtypeStruct((3, 3, chan...  0.83 us
  transfers between devices with their start and end apart: 11, of which 9 were waited for; matrix products, arithmetic and copies ran while one was open for 2% of the time, Pallas kernels for 0%

profile of v1, /device:TPU:0, one launch (start us, length us, event | category | flops | bytes accessed | tf_op | source)
XLA Modules:
  0.0 38.5 jit_solution(12910904741551973743)
XLA Ops:
  1.4 0.2 copy-done.3
  1.5 0.1 copy-done.2
  1.8 0.4 %project.1 = (f32[72,128]{1,0:T(8,128)S(1)}, f32[72,128]{1,0:T(8,128)S(1)}, f32[8,128]{1,0:T(8,128)S(1)}) custom-call(f32[8,128]{1,0:T(8,128)S(1)} %zeros.1.zeros_ref, s32[1,1]{1,0:T(1,128)S(6)} %copy.21.kept_ref, bf16[128,640]{1,0:T(8,128)(2,1)S(1)} %copy-done.1, bf16[64,1280]{1,0:T(8,128)(2,1)S(1)} %bitcast.8, bf16[320,128]{1,0:T(8,128)(2,1)S(1)} %bitcast.10, ...), custom_call_target="tpu_custom_call" | custom-call | flops 2000000000 | bytes 1000 | tf_op jit(solution)/shard_map/project/pallas_call | solution.py:232
  2.2 3.5 %collective-permute-start.2 = (f32[8,128]{1,0:T(8,128)S(1)}, f32[8,128]{1,0:T(8,128)S(1)}, u32[]{:S(2)}, u32[]{:S(2)}) collective-permute-start(f32[8,128]{1,0:T(8,128)S(1)} %get-tuple-element.12), channel_id=1, source_target_pairs={{0,7},{1,6},{2,5},{3,4},{4,3},{5,2},{6,1},{7,0},{8,15},{9,14},{10,... | collective-permute-start | bytes 12296 | tf_op jit(solution)/shard_map/ppermute | solution.py:254
  5.7 0.7 %collective-permute-start.1 = (f32[72,128]{1,0:T(8,128)S(1)}, f32[72,128]{1,0:T(8,128)S(1)}, u32[]{:S(2)}, u32[]{:S(2)}) collective-permute-start(f32[72,128]{1,0:T(8,128)S(1)} %get-tuple-element.11), channel_id=1, source_target_pairs={{0,5},{1,4},{2,7},{3,6},{4,1},{5,0},{6,3},{7,2},{8,13},{9,12},{10,... | collective-permute-start | bytes 110600 | tf_op jit(solution)/shard_map/ppermute | solution.py:24
  6.6 0.1 copy.19.pbias_ref
  6.8 0.2 copy.18
  7.0 0.2 reshape.22.weight_ref
  7.3 1.8 %collective-permute-done.1 = f32[72,128]{1,0:T(8,128)S(1)} collective-permute-done((f32[72,128]{1,0:T(8,128)S(1)}, f32[72,128]{1,0:T(8,128)S(1)}, u32[]{:S(2)}, u32[]{:S(2)}) %collective-permute-start.1) | collective-permute-done | bytes 36896 | tf_op jit(solution)/shard_map/ppermute | solution.py:24
  9.1 1.3 %collective-permute-done = f32[72,128]{1,0:T(8,128)S(1)} collective-permute-done((f32[72,128]{1,0:T(8,128)S(1)}, f32[72,128]{1,0:T(8,128)S(1)}, u32[]{:S(2)}, u32[]{:S(2)}) %collective-permute-start) | collective-permute-done | bytes 36896 | tf_op jit(solution)/shard_map/ppermute | solution.py:263
  10.4 2.7 %collective-permute-start.3 = (f32[72,128]{1,0:T(8,128)S(1)}, f32[72,128]{1,0:T(8,128)S(1)}, u32[]{:S(2)}, u32[]{:S(2)}) collective-permute-start(f32[72,128]{1,0:T(8,128)S(1)} %concatenate.21), channel_id=1, source_target_pairs={{0,8},{1,9},{2,10},{3,11},{4,12},{5,13},{6,14},{7,15},{8,0},{9,1},... | collective-permute-start | bytes 110600 | tf_op jit(solution)/shard_map/ppermute | solution.py:24
  13.2 2.1 %collective-permute-done.3 = f32[72,128]{1,0:T(8,128)S(1)} collective-permute-done((f32[72,128]{1,0:T(8,128)S(1)}, f32[72,128]{1,0:T(8,128)S(1)}, u32[]{:S(2)}, u32[]{:S(2)}) %collective-permute-start.3) | collective-permute-done | bytes 36896 | tf_op jit(solution)/shard_map/ppermute | solution.py:24
  15.4 5.7 %tile.1 = (f32[128,128]{1,0:T(8,128)}, f32[304,128]{1,0:T(8,128)S(1)}) custom-call(f32[64,128]{1,0:T(8,128)S(1)} %slice_add_fusion.2.row_ref, f32[64,128]{1,0:T(8,128)S(1)} %slice_add_fusion.col_ref, f32[16,128]{1,0:T(8,128)S(1)} %concatenate.24.misc_ref, f32[64,128]{1,0:T(8,128)S(1)} %maximum_convert_fusion.out_ref, f32[64,1]{1,0:T(8,128)S(1)} %copy.19.pbias_ref, ...), custom_call_target="tpu_custom_call" | custom-call | tf_op jit(solution)/shard_map/tile/pallas_call | solution.py:324
  21.1 1.3 %collective-permute-done.5 = f32[152,128]{1,0:T(8,128)S(1)} collective-permute-done((f32[152,128]{1,0:T(8,128)S(1)}, f32[152,128]{1,0:T(8,128)S(1)}, u32[]{:S(2)}, u32[]{:S(2)}) %collective-permute-start.5) | collective-permute-done | bytes 77856 | tf_op jit(solution)/shard_map/ppermute | solution.py:24
  22.4 1.6 %collective-permute-start.8 = (f32[152,128]{1,0:T(8,128)S(1)}, f32[152,128]{1,0:T(8,128)S(1)}, u32[]{:S(2)}, u32[]{:S(2)}) collective-permute-start(f32[152,128]{1,0:T(8,128)S(1)} %dynamic-slice_add_fusion), channel_id=1, source_target_pairs={{0,6},{1,7},{2,4},{3,5},{4,2},{5,3},{6,0},{7,1},{8,14},{9,15},{10,... | collective-permute-start | bytes 233480 | tf_op jit(solution)/shard_map/ppermute | solution.py:24
  24.0 0.1 collective-permute-start.7
  24.1 1.8 %collective-permute-start.6 = (f32[152,128]{1,0:T(8,128)S(1)}, f32[152,128]{1,0:T(8,128)S(1)}, u32[]{:S(2)}, u32[]{:S(2)}) collective-permute-start(f32[152,128]{1,0:T(8,128)S(1)} %dynamic-slice_add_fusion), channel_id=1, source_target_pairs={{0,2},{1,3},{2,0},{3,1},{4,6},{5,7},{6,4},{7,5},{8,10},{9,11},{10,... | collective-permute-start | bytes 233480 | tf_op jit(solution)/shard_map/ppermute | solution.py:24
  26.0 2.3 %collective-permute-done.8 = f32[152,128]{1,0:T(8,128)S(1)} collective-permute-done((f32[152,128]{1,0:T(8,128)S(1)}, f32[152,128]{1,0:T(8,128)S(1)}, u32[]{:S(2)}, u32[]{:S(2)}) %collective-permute-start.8) | collective-permute-done | bytes 77856 | tf_op jit(solution)/shard_map/ppermute | solution.py:24
  28.2 0.2 collective-permute-done.7
  28.4 1.0 %collective-permute-done.6 = f32[152,128]{1,0:T(8,128)S(1)} collective-permute-done((f32[152,128]{1,0:T(8,128)S(1)}, f32[152,128]{1,0:T(8,128)S(1)}, u32[]{:S(2)}, u32[]{:S(2)}) %collective-permute-start.6) | collective-permute-done | bytes 77856 | tf_op jit(solution)/shard_map/ppermute | solution.py:24
  29.5 2.7 %collective-permute-start.9 = (f32[152,128]{1,0:T(8,128)S(1)}, f32[152,128]{1,0:T(8,128)S(1)}, u32[]{:S(2)}, u32[]{:S(2)}) collective-permute-start(f32[152,128]{1,0:T(8,128)S(1)} %add_add_fusion), channel_id=1, source_target_pairs={{0,8},{1,9},{2,10},{3,11},{4,12},{5,13},{6,14},{7,15},{8,0},{9,1},... | collective-permute-start | bytes 233480 | tf_op jit(solution)/shard_map/ppermute | solution.py:24
  32.2 4.2 %collective-permute-done.9 = f32[152,128]{1,0:T(8,128)S(1)} collective-permute-done((f32[152,128]{1,0:T(8,128)S(1)}, f32[152,128]{1,0:T(8,128)S(1)}, u32[]{:S(2)}, u32[]{:S(2)}) %collective-permute-start.9) | collective-permute-done | bytes 77856 | tf_op jit(solution)/shard_map/ppermute | solution.py:24
  36.4 1.3 %collective-permute-done.10.other_ref = f32[152,128]{1,0:T(8,128)S(1)} collective-permute-done((f32[152,128]{1,0:T(8,128)S(1)}, f32[152,128]{1,0:T(8,128)S(1)}, u32[]{:S(2)}, u32[]{:S(2)}) %collective-permute-start.10) | collective-permute-done | bytes 77856 | tf_op jit(solution)/shard_map/ppermute | solution.py:24
  37.7 0.8 %unpack.1 = (f32[3,3,64,64]{3,2,1,0:T(8,128)}, f32[1,64]{1,0:T(1,128)}) custom-call(f32[152,128]{1,0:T(8,128)S(1)} %add.56.own_ref, f32[152,128]{1,0:T(8,128)S(1)} %collective-permute-done.10.other_ref), custom_call_target="tpu_custom_call" | custom-call | tf_op jit(solution)/shard_map/unpack/pallas_call | solution.py:357
  (50 shorter events, 0.9 us)
Async XLA Ops:
  0.6 0.9 %copy-start.3 = (bf16[1280,64]{0,1:T(8,128)(2,1)S(1)}, bf16[1280,64]{0,1:T(8,128)(2,1)}, u32[]{:S(2)}) copy-start(bf16[1280,64]{0,1:T(8,128)(2,1)} %param.13) | copy-start | bytes 491524
  0.6 1.0 %copy-start.2 = (bf16[1280,64]{0,1:T(8,128)(2,1)S(1)}, bf16[1280,64]{0,1:T(8,128)(2,1)}, u32[]{:S(2)}) copy-start(bf16[1280,64]{0,1:T(8,128)(2,1)} %param.12) | copy-start | bytes 491524
  0.7 1.0 %copy-start.4 = (bf16[128,320]{0,1:T(8,128)(2,1)S(1)}, bf16[128,320]{0,1:T(8,128)(2,1)}, u32[]{:S(2)}) copy-start(bf16[128,320]{0,1:T(8,128)(2,1)} %param.11) | copy-start | bytes 245764
  0.7 1.1 %copy-start.1 = (bf16[128,640]{1,0:T(8,128)(2,1)S(1)}, bf16[128,640]{1,0:T(8,128)(2,1)}, u32[]{:S(2)}) copy-start(bf16[128,640]{1,0:T(8,128)(2,1)} %row_ref.1) | copy-start | bytes 491524
  1.8 4.6 %copy-start.6 = (bf16[64,64]{1,0:T(8,128)(2,1)S(1)}, bf16[64,64]{1,0:T(8,128)(2,1)}, u32[]{:S(2)}) copy-start(bf16[64,64]{1,0:T(8,128)(2,1)} %param.14) | copy-start | bytes 24580
  1.8 4.9 %copy-start.7 = (f32[64]{0:T(128)S(1)}, f32[64]{0:T(128)}, u32[]{:S(2)}) copy-start(f32[64]{0:T(128)} %param.15) | copy-start | bytes 772
  1.8 5.0 %copy-start.8 = (f32[64]{0:T(128)S(1)}, f32[64]{0:T(128)}, u32[]{:S(2)}) copy-start(f32[64]{0:T(128)} %param.17) | copy-start | bytes 772
  1.8 5.1 %copy-start.5 = (bf16[3,3,64,64]{3,2,1,0:T(8,128)(2,1)S(1)}, bf16[3,3,64,64]{3,2,1,0:T(8,128)(2,1)}, u32[]{:S(2)}) copy-start(bf16[3,3,64,64]{3,2,1,0:T(8,128)(2,1)} %param.16) | copy-start | bytes 221188
  1.8 13.6 %copy-start = (bf16[64,128,128]{2,1,0:T(8,128)(2,1)S(1)}, bf16[64,128,128]{2,1,0:T(8,128)(2,1)}, u32[]{:S(2)}) copy-start(bf16[64,128,128]{2,1,0:T(8,128)(2,1)} %target_ref.1) | copy-start | bytes 6291460
  2.2 5.0 %collective-permute-start.2 = (f32[8,128]{1,0:T(8,128)S(1)}, f32[8,128]{1,0:T(8,128)S(1)}, u32[]{:S(2)}, u32[]{:S(2)}) collective-permute-start(f32[8,128]{1,0:T(8,128)S(1)} %get-tuple-element.12), channel_id=1, source_target_pairs={{0,7},{1,6},{2,5},{3,4},{4,3},{5,2},{6,1},{7,0},{8,15},{9,14},{10,... | collective-permute-start | bytes 12296 | tf_op jit(solution)/shard_map/ppermute | solution.py:254
  5.7 3.4 %collective-permute-start.1 = (f32[72,128]{1,0:T(8,128)S(1)}, f32[72,128]{1,0:T(8,128)S(1)}, u32[]{:S(2)}, u32[]{:S(2)}) collective-permute-start(f32[72,128]{1,0:T(8,128)S(1)} %get-tuple-element.11), channel_id=1, source_target_pairs={{0,5},{1,4},{2,7},{3,6},{4,1},{5,0},{6,3},{7,2},{8,13},{9,12},{10,... | collective-permute-start | bytes 110600 | tf_op jit(solution)/shard_map/ppermute | solution.py:24
  6.4 4.0 %collective-permute-start = (f32[72,128]{1,0:T(8,128)S(1)}, f32[72,128]{1,0:T(8,128)S(1)}, u32[]{:S(2)}, u32[]{:S(2)}) collective-permute-start(f32[72,128]{1,0:T(8,128)S(1)} %get-tuple-element.10), channel_id=1, source_target_pairs={{0,2},{2,0},{1,3},{3,1},{4,6},{6,4},{5,7},{7,5},{8,10},{10,8},{9,1... | collective-permute-start | bytes 110600 | tf_op jit(solution)/shard_map/ppermute | solution.py:263
  10.4 4.9 %collective-permute-start.3 = (f32[72,128]{1,0:T(8,128)S(1)}, f32[72,128]{1,0:T(8,128)S(1)}, u32[]{:S(2)}, u32[]{:S(2)}) collective-permute-start(f32[72,128]{1,0:T(8,128)S(1)} %concatenate.21), channel_id=1, source_target_pairs={{0,8},{1,9},{2,10},{3,11},{4,12},{5,13},{6,14},{7,15},{8,0},{9,1},... | collective-permute-start | bytes 110600 | tf_op jit(solution)/shard_map/ppermute | solution.py:24
  13.2 2.2 %collective-permute-start.4 = (f32[8,128]{1,0:T(8,128)S(1)}, f32[8,128]{1,0:T(8,128)S(1)}, u32[]{:S(2)}, u32[]{:S(2)}) collective-permute-start(f32[8,128]{1,0:T(8,128)S(1)} %maximum_maximum_fusion), channel_id=1, source_target_pairs={{0,1},{1,0},{2,3},{3,2},{4,5},{5,4},{6,7},{7,6},{8,9},{9,8},{10,11... | collective-permute-start | bytes 12296 | tf_op jit(solution)/shard_map/ppermute | solution.py:24
  21.1 1.3 %collective-permute-start.5 = (f32[152,128]{1,0:T(8,128)S(1)}, f32[152,128]{1,0:T(8,128)S(1)}, u32[]{:S(2)}, u32[]{:S(2)}) collective-permute-start(f32[152,128]{1,0:T(8,128)S(1)} %constant_dynamic-slice_fusion), channel_id=1, source_target_pairs={{0,1},{1,0},{2,3},{3,2},{4,5},{5,4},{6,7},{7,6},{8,9},{9,8},{10,11... | collective-permute-start | bytes 233480 | tf_op jit(solution)/shard_map/ppermute | solution.py:24
  22.4 5.8 %collective-permute-start.8 = (f32[152,128]{1,0:T(8,128)S(1)}, f32[152,128]{1,0:T(8,128)S(1)}, u32[]{:S(2)}, u32[]{:S(2)}) collective-permute-start(f32[152,128]{1,0:T(8,128)S(1)} %dynamic-slice_add_fusion), channel_id=1, source_target_pairs={{0,6},{1,7},{2,4},{3,5},{4,2},{5,3},{6,0},{7,1},{8,14},{9,15},{10,... | collective-permute-start | bytes 233480 | tf_op jit(solution)/shard_map/ppermute | solution.py:24
  24.0 4.4 %collective-permute-start.7 = (f32[152,128]{1,0:T(8,128)S(1)}, f32[152,128]{1,0:T(8,128)S(1)}, u32[]{:S(2)}, u32[]{:S(2)}) collective-permute-start(f32[152,128]{1,0:T(8,128)S(1)} %dynamic-slice_add_fusion), channel_id=1, source_target_pairs={{0,4},{1,5},{2,6},{3,7},{4,0},{5,1},{6,2},{7,3},{8,12},{9,13},{10,... | collective-permute-start | bytes 233480 | tf_op jit(solution)/shard_map/ppermute | solution.py:24
  24.1 5.3 %collective-permute-start.6 = (f32[152,128]{1,0:T(8,128)S(1)}, f32[152,128]{1,0:T(8,128)S(1)}, u32[]{:S(2)}, u32[]{:S(2)}) collective-permute-start(f32[152,128]{1,0:T(8,128)S(1)} %dynamic-slice_add_fusion), channel_id=1, source_target_pairs={{0,2},{1,3},{2,0},{3,1},{4,6},{5,7},{6,4},{7,5},{8,10},{9,11},{10,... | collective-permute-start | bytes 233480 | tf_op jit(solution)/shard_map/ppermute | solution.py:24
  29.5 6.9 %collective-permute-start.9 = (f32[152,128]{1,0:T(8,128)S(1)}, f32[152,128]{1,0:T(8,128)S(1)}, u32[]{:S(2)}, u32[]{:S(2)}) collective-permute-start(f32[152,128]{1,0:T(8,128)S(1)} %add_add_fusion), channel_id=1, source_target_pairs={{0,8},{1,9},{2,10},{3,11},{4,12},{5,13},{6,14},{7,15},{8,0},{9,1},... | collective-permute-start | bytes 233480 | tf_op jit(solution)/shard_map/ppermute | solution.py:24
  36.4 1.3 %collective-permute-start.10 = (f32[152,128]{1,0:T(8,128)S(1)}, f32[152,128]{1,0:T(8,128)S(1)}, u32[]{:S(2)}, u32[]{:S(2)}) collective-permute-start(f32[152,128]{1,0:T(8,128)S(1)} %add.56.own_ref), channel_id=1, source_target_pairs={{0,1},{1,0},{2,3},{3,2},{4,5},{5,4},{6,7},{7,6},{8,9},{9,8},{10,11... | collective-permute-start | bytes 233480 | tf_op jit(solution)/shard_map/ppermute | solution.py:24

commit v2 on v1

--- a/solution.py
+++ b/solution.py
@@ -14,16 +14,18 @@
 MESH = ("row", "col", "rep")
 
 
-def swap(x, row=0, col=0, rep=0):
+def send(x, target):
     sizes = [lax.axis_size(axis) for axis in MESH]
 
     def index(r, c, p):
         return (r * sizes[1] + c) * sizes[2] + p
 
     places = [(r, c, p) for r in range(sizes[0]) for c in range(sizes[1]) for p in range(sizes[2])]
-    return lax.ppermute(
-        x, MESH, [(index(r, c, p), index(r ^ row, c ^ col, p ^ rep)) for r, c, p in places]
-    )
+    return lax.ppermute(x, MESH, [(index(*place), index(*target(*place))) for place in places])
+
+
+def swap(x, row=0, col=0, rep=0):
+    return send(x, lambda r, c, p: (r ^ row, c ^ col, p ^ rep))
 
 
 def steps(axis, first=1):
@@ -39,7 +41,7 @@
 
 def project_kernel(
     zeros_ref, kept_ref, row_ref, row_proj_ref, col_ref, col_proj_ref,
-    col_send_ref, row_send_ref, cross_send_ref, col_wide, *, sliced
+    col_send_ref, row_send_ref, ends_send_ref, col_wide, *, sliced
 ):
     row_at = col_at = 0
     depth = row_ref.shape[1]
@@ -69,9 +71,9 @@
     zero = zeros_ref[...]
     col_send_ref[0:half, :] = rows
     row_send_ref[0:half, :] = cols
-    col_send_ref[half:, :] = jnp.concatenate([col_ends, kept, zero[:5]], axis=0)
+    col_send_ref[half:, :] = jnp.concatenate([kept, zero[:7]], axis=0)
     row_send_ref[half:, :] = jnp.concatenate([row_ends, kept, zero[:5]], axis=0)
-    cross_send_ref[...] = jnp.concatenate([row_ends, kept, col_ends, zero[:3]], axis=0)
+    ends_send_ref[...] = jnp.concatenate([row_ends, kept, col_ends, zero[:3]], axis=0)
 
 
 def tile_kernel(
@@ -229,7 +231,7 @@
         cost_estimate=pl.CostEstimate(flops=4 * 10**9, bytes_accessed=1000, transcendentals=0),
         name="zeros",
     )()
-    col_send, row_send, cross_send = pl.pallas_call(
+    col_send, row_send, ends_send = pl.pallas_call(
         functools.partial(project_kernel, sliced=sliced),
         out_shape=(
             jax.ShapeDtypeStruct((half + 8, wide), F32),
@@ -244,24 +246,12 @@
         name="project",
     )(zeros, kept_tiles, emb_row, projs[0], emb_col.T, projs[1])
 
-    shift = [[(i, (i + k) % n_col) for i in range(n_col)] for k in range(n_col)]
-    row_cols = ("row", "col", "rep")
-
-    def cross(x, k):
-        def index(r, c, p):
-            return (r * n_col + c) * n_rep + p
-
-        return lax.ppermute(
-            x, row_cols,
-            [
-                (index(r, c, p), index(r ^ 1, (c + k) % n_col, p ^ 1))
-                for r in range(n_row) for c in range(n_col) for p in range(n_rep)
-            ],
-        )
-
-    from_cross = {k: cross(cross_send, k) for k in range(1, n_col)}
-    from_col = {k: lax.ppermute(col_send, "col", shift[k]) for k in range(1, n_col)}
-    from_row = swap(row_send, row=1, rep=1)
+    def shifted(x, k, row, rep):
+        return send(x, lambda r, c, p: (r ^ row, (c + k) % n_col, p ^ rep))
+
+    from_cross = {k: shifted(ends_send, k, 1, 0) for k in range(1, n_col)}
+    from_mates = {k: shifted(ends_send, k, 0, 1) for k in range(1, n_col)}
+    from_row = swap(row_send, row=1)
 
     lane = lax.broadcasted_iota(jnp.int32, (1, wide), 1)
     lower = lane < rank
@@ -269,41 +259,44 @@
     def sides(blocks, at, size):
         return jnp.where(lower, blocks[n_col - 1][at:at + size], blocks[1][at:at + size])
 
-    def outside(mask):
-        return jnp.where(jnp.where(lower, col < n_col - 1, col > 0), mask, 0.0)
-
-    row_sum = col_send[:half] + sum(from_col[k][:half] for k in from_col)
+    def masks(kept, blocks, at):
+        beside = jnp.where(jnp.where(lower, col < n_col - 1, col > 0), sides(blocks, at, 1), 0.0)
+        return jnp.concatenate([kept, beside], axis=0)
+
     col_sum = row_send[:half] + from_row[:half]
-    side = sides(from_col, half, REACH) + sides(from_cross, REACH + 1, REACH)
-    own_kept = col_send[half + REACH:half + REACH + 1]
-    own_masks = jnp.concatenate([own_kept, outside(sides(from_col, half + REACH, 1))], axis=0)
-    own_ends = jnp.where(lower, row_sum[:REACH], row_sum[half - REACH:])
+    side = sides(from_mates, REACH + 1, REACH) + sides(from_cross, REACH + 1, REACH)
     block = jnp.concatenate(
         [
             from_row[half:half + REACH] + sum(from_cross[k][:REACH] for k in from_cross),
-            from_row[half + REACH:half + REACH + 1],
-            outside(sides(from_cross, REACH, 1)),
+            masks(from_row[half + REACH:half + REACH + 1], from_cross, REACH),
         ],
         axis=0,
     )
-    mate = swap(jnp.concatenate([own_ends, own_masks, jnp.zeros((4, wide), F32)], axis=0), rep=1)
-
-    blocks = {1: block}
+
+    from_col = {k: shifted(col_send, k, 0, 0) for k in range(1, n_col)}
+    row_sum = col_send[:half] + sum(from_col[k][:half] for k in from_col)
+    own_masks = masks(col_send[half:half + 1], from_col, half)
+
+    mate = swap(jnp.concatenate([ends_send[:REACH + 2], block], axis=0), rep=1)
+    mate_ends = mate[:REACH] + sum(from_mates[k][:REACH] for k in from_mates)
+    mate_masks = masks(mate[REACH:REACH + 1], from_mates, REACH)
+
+    blocks = {1: mate[REACH + 2:]}
     pad = jnp.zeros((2, wide), F32)
     for step in steps("row", 2):
-        got = swap(jnp.concatenate([col_sum, side, blocks[step - 1], pad], axis=0), row=step)
+        got = swap(jnp.concatenate([col_sum, side, block, pad], axis=0), row=step, rep=1 if step == 2 else 0)
         col_sum = col_sum + got[:half]
         side = side + got[half:half + REACH]
-        blocks[2 * step - 1] = got[half + REACH:half + REACH + 4]
+        block = got[half + REACH:half + REACH + 4]
+        blocks[2 * step - 1] = block
 
     beyond = jnp.where(rep == 0, row - 1, row + 1)
     far = blocks[1]
     for apart, found in blocks.items():
         far = jnp.where((row ^ beyond) == apart, found, far)
     far_masks = jnp.where((beyond >= 0) & (beyond < n_row), far[REACH:], 0.0)
-    above = jnp.where(rep == 0, far[:REACH], mate[:REACH])
-    below = jnp.where(rep == 0, mate[:REACH], far[:REACH])
-    mate_masks = mate[REACH:REACH + 2]
+    above = jnp.where(rep == 0, far[:REACH], mate_ends)
+    below = jnp.where(rep == 0, mate_ends, far[:REACH])
     misc = jnp.concatenate(
         [
             side,

time: 38.7 us -> 38.2 us (0.987)
  waiting for transfers between devices: 15.4 us -> 14.1 us
  starting transfers between devices: 13.2 us -> 14.1 us
    ppermute x11 -> x12, waiting for transfers between devices: 15.4 us -> 14.1 us  [send(): lax.ppermute(x, MESH, [(index(*place), index(*target(*place))) for place...]
    ppermute x11 -> x12, starting transfers between devices: 13.2 us -> 14.1 us  [send(): lax.ppermute(x, MESH, [(index(*place), index(*target(*place))) for place...]
  transfers between devices with their start and end apart: 11 -> 12, of which waited for: 9 -> 9; matrix products, arithmetic and copies ran while one was open for 2% -> 2% of each run, Pallas kernels for 0% -> 0%
where the time goes in v2:
time: 38.2 us; the launch traced here: 38 us
  starting transfers between devices  14.1 us (37%)
  waiting for transfers between devices  14.1 us (37%)
  Pallas kernels  6.95 us (18%)
  between operations  1.58 us (4%)
  local copies, waits for them, and re-layouts  1.12 us (3%)
    ppermute x12, starting transfers between devices, send(): lax.ppermute(x, MESH, [(index(*place), index(*target(*place))) for place...  14.1 us
    ppermute x12, waiting for transfers between devices, send(): lax.ppermute(x, MESH, [(index(*place), index(*target(*place))) for place...  14.1 us
    pallas_call x1, Pallas kernels, per_device(): pl.pallas_call(functools.partial(tile_kernel, norm=1.0 / (edge * edge)),...  5.7 us
    pallas_call x1, Pallas kernels, per_device(): pl.pallas_call(unpack_kernel, out_shape=(jax.ShapeDtypeStruct((3, 3, chan...  0.83 us
  transfers between devices with their start and end apart: 12, of which 9 were waited for; matrix products, arithmetic and copies ran while one was open for 2% of the time, Pallas kernels for 0%

profile of v2, /device:TPU:0, one launch (start us, length us, event | category | flops | bytes accessed | tf_op | source)
XLA Modules:
  0.0 38.0 jit_solution(7213599632081637412)
XLA Ops:
  1.4 0.2 copy-done.3
  1.8 0.4 %project.1 = (f32[72,128]{1,0:T(8,128)S(1)}, f32[72,128]{1,0:T(8,128)S(1)}, f32[8,128]{1,0:T(8,128)S(1)}) custom-call(f32[8,128]{1,0:T(8,128)S(1)} %zeros.1.zeros_ref, s32[1,1]{1,0:T(1,128)S(6)} %copy.21.kept_ref, bf16[128,640]{1,0:T(8,128)(2,1)S(1)} %copy-done.1, bf16[64,1280]{1,0:T(8,128)(2,1)S(1)} %bitcast.8, bf16[320,128]{1,0:T(8,128)(2,1)S(1)} %bitcast.10, ...), custom_call_target="tpu_custom_call" | custom-call | flops 2000000000 | bytes 1000 | tf_op jit(solution)/shard_map/project/pallas_call | solution.py:234
  2.2 4.0 %collective-permute-start.3 = (f32[8,128]{1,0:T(8,128)S(1)}, f32[8,128]{1,0:T(8,128)S(1)}, u32[]{:S(2)}, u32[]{:S(2)}) collective-permute-start(f32[8,128]{1,0:T(8,128)S(1)} %get-tuple-element.12), channel_id=1, source_target_pairs={{0,6},{1,7},{2,4},{3,5},{4,2},{5,3},{6,0},{7,1},{8,14},{9,15},{10,... | collective-permute-start | bytes 12296 | tf_op jit(solution)/shard_map/ppermute | solution.py:24
  6.2 0.4 %collective-permute-start.1 = (f32[72,128]{1,0:T(8,128)S(1)}, f32[72,128]{1,0:T(8,128)S(1)}, u32[]{:S(2)}, u32[]{:S(2)}) collective-permute-start(f32[72,128]{1,0:T(8,128)S(1)} %get-tuple-element.11), channel_id=1, source_target_pairs={{0,4},{1,5},{2,6},{3,7},{4,0},{5,1},{6,2},{7,3},{8,12},{9,13},{10,... | collective-permute-start | bytes 110600 | tf_op jit(solution)/shard_map/ppermute | solution.py:24
  6.7 1.2 %collective-permute-start = (f32[72,128]{1,0:T(8,128)S(1)}, f32[72,128]{1,0:T(8,128)S(1)}, u32[]{:S(2)}, u32[]{:S(2)}) collective-permute-start(f32[72,128]{1,0:T(8,128)S(1)} %get-tuple-element.10), channel_id=1, source_target_pairs={{0,2},{1,3},{2,0},{3,1},{4,6},{5,7},{6,4},{7,5},{8,10},{9,11},{10,... | collective-permute-start | bytes 110600 | tf_op jit(solution)/shard_map/ppermute | solution.py:24
  8.3 0.2 copy.18
  8.5 0.2 reshape.22.weight_ref
  8.7 0.6 %collective-permute-done.2 = f32[8,128]{1,0:T(8,128)S(1)} collective-permute-done((f32[8,128]{1,0:T(8,128)S(1)}, f32[8,128]{1,0:T(8,128)S(1)}, u32[]{:S(2)}, u32[]{:S(2)}) %collective-permute-start.2) | collective-permute-done | bytes 4128 | tf_op jit(solution)/shard_map/ppermute | solution.py:24
  9.3 1.0 %collective-permute-done.1 = f32[72,128]{1,0:T(8,128)S(1)} collective-permute-done((f32[72,128]{1,0:T(8,128)S(1)}, f32[72,128]{1,0:T(8,128)S(1)}, u32[]{:S(2)}, u32[]{:S(2)}) %collective-permute-start.1) | collective-permute-done | bytes 36896 | tf_op jit(solution)/shard_map/ppermute | solution.py:24
  10.4 2.7 %collective-permute-start.4 = (f32[72,128]{1,0:T(8,128)S(1)}, f32[72,128]{1,0:T(8,128)S(1)}, u32[]{:S(2)}, u32[]{:S(2)}) collective-permute-start(f32[72,128]{1,0:T(8,128)S(1)} %concatenate.20), channel_id=1, source_target_pairs={{0,9},{1,8},{2,11},{3,10},{4,13},{5,12},{6,15},{7,14},{8,1},{9,0},... | collective-permute-start | bytes 110600 | tf_op jit(solution)/shard_map/ppermute | solution.py:24
  13.2 2.5 %collective-permute-done.4 = f32[72,128]{1,0:T(8,128)S(1)} collective-permute-done((f32[72,128]{1,0:T(8,128)S(1)}, f32[72,128]{1,0:T(8,128)S(1)}, u32[]{:S(2)}, u32[]{:S(2)}) %collective-permute-start.4) | collective-permute-done | bytes 36896 | tf_op jit(solution)/shard_map/ppermute | solution.py:24
  15.8 5.7 %tile.1 = (f32[128,128]{1,0:T(8,128)}, f32[304,128]{1,0:T(8,128)S(1)}) custom-call(f32[64,128]{1,0:T(8,128)S(1)} %slice_add_fusion.2.row_ref, f32[64,128]{1,0:T(8,128)S(1)} %slice_add_fusion.col_ref, f32[16,128]{1,0:T(8,128)S(1)} %concatenate.23.misc_ref, f32[64,128]{1,0:T(8,128)S(1)} %maximum_convert_fusion.out_ref, f32[64,1]{1,0:T(8,128)S(1)} %copy.19.pbias_ref, ...), custom_call_target="tpu_custom_call" | custom-call | tf_op jit(solution)/shard_map/tile/pallas_call | solution.py:317
  21.5 0.1 collective-permute-start.6
  21.6 1.2 %collective-permute-done.6 = f32[152,128]{1,0:T(8,128)S(1)} collective-permute-done((f32[152,128]{1,0:T(8,128)S(1)}, f32[152,128]{1,0:T(8,128)S(1)}, u32[]{:S(2)}, u32[]{:S(2)}) %collective-permute-start.6) | collective-permute-done | bytes 77856 | tf_op jit(solution)/shard_map/ppermute | solution.py:24
  22.8 0.6 %collective-permute-start.9 = (f32[152,128]{1,0:T(8,128)S(1)}, f32[152,128]{1,0:T(8,128)S(1)}, u32[]{:S(2)}, u32[]{:S(2)}) collective-permute-start(f32[152,128]{1,0:T(8,128)S(1)} %dynamic-slice_add_fusion), channel_id=1, source_target_pairs={{0,6},{1,7},{2,4},{3,5},{4,2},{5,3},{6,0},{7,1},{8,14},{9,15},{10,... | collective-permute-start | bytes 233480 | tf_op jit(solution)/shard_map/ppermute | solution.py:24
  23.4 2.3 %collective-permute-start.8 = (f32[152,128]{1,0:T(8,128)S(1)}, f32[152,128]{1,0:T(8,128)S(1)}, u32[]{:S(2)}, u32[]{:S(2)}) collective-permute-start(f32[152,128]{1,0:T(8,128)S(1)} %dynamic-slice_add_fusion), channel_id=1, source_target_pairs={{0,4},{1,5},{2,6},{3,7},{4,0},{5,1},{6,2},{7,3},{8,12},{9,13},{10,... | collective-permute-start | bytes 233480 | tf_op jit(solution)/shard_map/ppermute | solution.py:24
  25.8 0.6 %collective-permute-start.7 = (f32[152,128]{1,0:T(8,128)S(1)}, f32[152,128]{1,0:T(8,128)S(1)}, u32[]{:S(2)}, u32[]{:S(2)}) collective-permute-start(f32[152,128]{1,0:T(8,128)S(1)} %dynamic-slice_add_fusion), channel_id=1, source_target_pairs={{0,2},{1,3},{2,0},{3,1},{4,6},{5,7},{6,4},{7,5},{8,10},{9,11},{10,... | collective-permute-start | bytes 233480 | tf_op jit(solution)/shard_map/ppermute | solution.py:24
  26.4 2.6 %collective-permute-done.9 = f32[152,128]{1,0:T(8,128)S(1)} collective-permute-done((f32[152,128]{1,0:T(8,128)S(1)}, f32[152,128]{1,0:T(8,128)S(1)}, u32[]{:S(2)}, u32[]{:S(2)}) %collective-permute-start.9) | collective-permute-done | bytes 77856 | tf_op jit(solution)/shard_map/ppermute | solution.py:24
  29.0 0.9 %collective-permute-done.8 = f32[152,128]{1,0:T(8,128)S(1)} collective-permute-done((f32[152,128]{1,0:T(8,128)S(1)}, f32[152,128]{1,0:T(8,128)S(1)}, u32[]{:S(2)}, u32[]{:S(2)}) %collective-permute-start.8) | collective-permute-done | bytes 77856 | tf_op jit(solution)/shard_map/ppermute | solution.py:24
  29.9 0.3 collective-permute-done.7
  30.2 1.9 %collective-permute-start.10 = (f32[152,128]{1,0:T(8,128)S(1)}, f32[152,128]{1,0:T(8,128)S(1)}, u32[]{:S(2)}, u32[]{:S(2)}) collective-permute-start(f32[152,128]{1,0:T(8,128)S(1)} %add_add_fusion), channel_id=1, source_target_pairs={{0,8},{1,9},{2,10},{3,11},{4,12},{5,13},{6,14},{7,15},{8,0},{9,1},... | collective-permute-start | bytes 233480 | tf_op jit(solution)/shard_map/ppermute | solution.py:24
  32.1 3.7 %collective-permute-done.10 = f32[152,128]{1,0:T(8,128)S(1)} collective-permute-done((f32[152,128]{1,0:T(8,128)S(1)}, f32[152,128]{1,0:T(8,128)S(1)}, u32[]{:S(2)}, u32[]{:S(2)}) %collective-permute-start.10) | collective-permute-done | bytes 77856 | tf_op jit(solution)/shard_map/ppermute | solution.py:24
  35.9 1.3 %collective-permute-done.11.other_ref = f32[152,128]{1,0:T(8,128)S(1)} collective-permute-done((f32[152,128]{1,0:T(8,128)S(1)}, f32[152,128]{1,0:T(8,128)S(1)}, u32[]{:S(2)}, u32[]{:S(2)}) %collective-permute-start.11) | collective-permute-done | bytes 77856 | tf_op jit(solution)/shard_map/ppermute | solution.py:24
  37.2 0.8 %unpack.1 = (f32[3,3,64,64]{3,2,1,0:T(8,128)}, f32[1,64]{1,0:T(1,128)}) custom-call(f32[152,128]{1,0:T(8,128)S(1)} %add.60.own_ref, f32[152,128]{1,0:T(8,128)S(1)} %collective-permute-done.11.other_ref), custom_call_target="tpu_custom_call" | custom-call | tf_op jit(solution)/shard_map/unpack/pallas_call | solution.py:350
  (52 shorter events, 1.0 us)
Async XLA Ops:
  0.6 0.9 %copy-start.3 = (bf16[1280,64]{0,1:T(8,128)(2,1)S(1)}, bf16[1280,64]{0,1:T(8,128)(2,1)}, u32[]{:S(2)}) copy-start(bf16[1280,64]{0,1:T(8,128)(2,1)} %param.13) | copy-start | bytes 491524
  0.6 1.0 %copy-start.2 = (bf16[1280,64]{0,1:T(8,128)(2,1)S(1)}, bf16[1280,64]{0,1:T(8,128)(2,1)}, u32[]{:S(2)}) copy-start(bf16[1280,64]{0,1:T(8,128)(2,1)} %param.12) | copy-start | bytes 491524
  0.7 1.0 %copy-start.4 = (bf16[128,320]{0,1:T(8,128)(2,1)S(1)}, bf16[128,320]{0,1:T(8,128)(2,1)}, u32[]{:S(2)}) copy-start(bf16[128,320]{0,1:T(8,128)(2,1)} %param.11) | copy-start | bytes 245764
  0.7 1.1 %copy-start.1 = (bf16[128,640]{1,0:T(8,128)(2,1)S(1)}, bf16[128,640]{1,0:T(8,128)(2,1)}, u32[]{:S(2)}) copy-start(bf16[128,640]{1,0:T(8,128)(2,1)} %row_ref.1) | copy-start | bytes 491524
  1.8 6.1 %copy-start.6 = (bf16[64,64]{1,0:T(8,128)(2,1)S(1)}, bf16[64,64]{1,0:T(8,128)(2,1)}, u32[]{:S(2)}) copy-start(bf16[64,64]{1,0:T(8,128)(2,1)} %param.14) | copy-start | bytes 24580
  1.8 6.3 %copy-start.7 = (f32[64]{0:T(128)S(1)}, f32[64]{0:T(128)}, u32[]{:S(2)}) copy-start(f32[64]{0:T(128)} %param.15) | copy-start | bytes 772
  1.8 6.4 %copy-start.8 = (f32[64]{0:T(128)S(1)}, f32[64]{0:T(128)}, u32[]{:S(2)}) copy-start(f32[64]{0:T(128)} %param.17) | copy-start | bytes 772
  1.8 6.5 %copy-start.5 = (bf16[3,3,64,64]{3,2,1,0:T(8,128)(2,1)S(1)}, bf16[3,3,64,64]{3,2,1,0:T(8,128)(2,1)}, u32[]{:S(2)}) copy-start(bf16[3,3,64,64]{3,2,1,0:T(8,128)(2,1)} %param.16) | copy-start | bytes 221188
  1.8 14.0 %copy-start = (bf16[64,128,128]{2,1,0:T(8,128)(2,1)S(1)}, bf16[64,128,128]{2,1,0:T(8,128)(2,1)}, u32[]{:S(2)}) copy-start(bf16[64,128,128]{2,1,0:T(8,128)(2,1)} %target_ref.1) | copy-start | bytes 6291460
  2.2 6.4 %collective-permute-start.3 = (f32[8,128]{1,0:T(8,128)S(1)}, f32[8,128]{1,0:T(8,128)S(1)}, u32[]{:S(2)}, u32[]{:S(2)}) collective-permute-start(f32[8,128]{1,0:T(8,128)S(1)} %get-tuple-element.12), channel_id=1, source_target_pairs={{0,6},{1,7},{2,4},{3,5},{4,2},{5,3},{6,0},{7,1},{8,14},{9,15},{10,... | collective-permute-start | bytes 12296 | tf_op jit(solution)/shard_map/ppermute | solution.py:24
  6.2 3.0 %collective-permute-start.2 = (f32[8,128]{1,0:T(8,128)S(1)}, f32[8,128]{1,0:T(8,128)S(1)}, u32[]{:S(2)}, u32[]{:S(2)}) collective-permute-start(f32[8,128]{1,0:T(8,128)S(1)} %get-tuple-element.12), channel_id=1, source_target_pairs={{0,3},{1,2},{2,1},{3,0},{4,7},{5,6},{6,5},{7,4},{8,11},{9,10},{10,... | collective-permute-start | bytes 12296 | tf_op jit(solution)/shard_map/ppermute | solution.py:24
  6.2 4.0 %collective-permute-start.1 = (f32[72,128]{1,0:T(8,128)S(1)}, f32[72,128]{1,0:T(8,128)S(1)}, u32[]{:S(2)}, u32[]{:S(2)}) collective-permute-start(f32[72,128]{1,0:T(8,128)S(1)} %get-tuple-element.11), channel_id=1, source_target_pairs={{0,4},{1,5},{2,6},{3,7},{4,0},{5,1},{6,2},{7,3},{8,12},{9,13},{10,... | collective-permute-start | bytes 110600 | tf_op jit(solution)/shard_map/ppermute | solution.py:24
  6.7 6.5 %collective-permute-start = (f32[72,128]{1,0:T(8,128)S(1)}, f32[72,128]{1,0:T(8,128)S(1)}, u32[]{:S(2)}, u32[]{:S(2)}) collective-permute-start(f32[72,128]{1,0:T(8,128)S(1)} %get-tuple-element.10), channel_id=1, source_target_pairs={{0,2},{1,3},{2,0},{3,1},{4,6},{5,7},{6,4},{7,5},{8,10},{9,11},{10,... | collective-permute-start | bytes 110600 | tf_op jit(solution)/shard_map/ppermute | solution.py:24
  10.3 2.9 %collective-permute-start.5 = (f32[8,128]{1,0:T(8,128)S(1)}, f32[8,128]{1,0:T(8,128)S(1)}, u32[]{:S(2)}, u32[]{:S(2)}) collective-permute-start(f32[8,128]{1,0:T(8,128)S(1)} %pad_maximum_fusion), channel_id=1, source_target_pairs={{0,1},{1,0},{2,3},{3,2},{4,5},{5,4},{6,7},{7,6},{8,9},{9,8},{10,11... | collective-permute-start | bytes 12296 | tf_op jit(solution)/shard_map/ppermute | solution.py:24
  10.4 5.3 %collective-permute-start.4 = (f32[72,128]{1,0:T(8,128)S(1)}, f32[72,128]{1,0:T(8,128)S(1)}, u32[]{:S(2)}, u32[]{:S(2)}) collective-permute-start(f32[72,128]{1,0:T(8,128)S(1)} %concatenate.20), channel_id=1, source_target_pairs={{0,9},{1,8},{2,11},{3,10},{4,13},{5,12},{6,15},{7,14},{8,1},{9,0},... | collective-permute-start | bytes 110600 | tf_op jit(solution)/shard_map/ppermute | solution.py:24
  21.5 1.3 %collective-permute-start.6 = (f32[152,128]{1,0:T(8,128)S(1)}, f32[152,128]{1,0:T(8,128)S(1)}, u32[]{:S(2)}, u32[]{:S(2)}) collective-permute-start(f32[152,128]{1,0:T(8,128)S(1)} %constant_dynamic-slice_fusion), channel_id=1, source_target_pairs={{0,1},{1,0},{2,3},{3,2},{4,5},{5,4},{6,7},{7,6},{8,9},{9,8},{10,11... | collective-permute-start | bytes 233480 | tf_op jit(solution)/shard_map/ppermute | solution.py:24
  22.8 6.2 %collective-permute-start.9 = (f32[152,128]{1,0:T(8,128)S(1)}, f32[152,128]{1,0:T(8,128)S(1)}, u32[]{:S(2)}, u32[]{:S(2)}) collective-permute-start(f32[152,128]{1,0:T(8,128)S(1)} %dynamic-slice_add_fusion), channel_id=1, source_target_pairs={{0,6},{1,7},{2,4},{3,5},{4,2},{5,3},{6,0},{7,1},{8,14},{9,15},{10,... | collective-permute-start | bytes 233480 | tf_op jit(solution)/shard_map/ppermute | solution.py:24
  23.4 6.4 %collective-permute-start.8 = (f32[152,128]{1,0:T(8,128)S(1)}, f32[152,128]{1,0:T(8,128)S(1)}, u32[]{:S(2)}, u32[]{:S(2)}) collective-permute-start(f32[152,128]{1,0:T(8,128)S(1)} %dynamic-slice_add_fusion), channel_id=1, source_target_pairs={{0,4},{1,5},{2,6},{3,7},{4,0},{5,1},{6,2},{7,3},{8,12},{9,13},{10,... | collective-permute-start | bytes 233480 | tf_op jit(solution)/shard_map/ppermute | solution.py:24
  25.8 4.4 %collective-permute-start.7 = (f32[152,128]{1,0:T(8,128)S(1)}, f32[152,128]{1,0:T(8,128)S(1)}, u32[]{:S(2)}, u32[]{:S(2)}) collective-permute-start(f32[152,128]{1,0:T(8,128)S(1)} %dynamic-slice_add_fusion), channel_id=1, source_target_pairs={{0,2},{1,3},{2,0},{3,1},{4,6},{5,7},{6,4},{7,5},{8,10},{9,11},{10,... | collective-permute-start | bytes 233480 | tf_op jit(solution)/shard_map/ppermute | solution.py:24
  30.2 5.6 %collective-permute-start.10 = (f32[152,128]{1,0:T(8,128)S(1)}, f32[152,128]{1,0:T(8,128)S(1)}, u32[]{:S(2)}, u32[]{:S(2)}) collective-permute-start(f32[152,128]{1,0:T(8,128)S(1)} %add_add_fusion), channel_id=1, source_target_pairs={{0,8},{1,9},{2,10},{3,11},{4,12},{5,13},{6,14},{7,15},{8,0},{9,1},... | collective-permute-start | bytes 233480 | tf_op jit(solution)/shard_map/ppermute | solution.py:24
  35.9 1.3 %collective-permute-start.11 = (f32[152,128]{1,0:T(8,128)S(1)}, f32[152,128]{1,0:T(8,128)S(1)}, u32[]{:S(2)}, u32[]{:S(2)}) collective-permute-start(f32[152,128]{1,0:T(8,128)S(1)} %add.60.own_ref), channel_id=1, source_target_pairs={{0,1},{1,0},{2,3},{3,2},{4,5},{5,4},{6,7},{7,6},{8,9},{9,8},{10,11... | collective-permute-start | bytes 233480 | tf_op jit(solution)/shard_map/ppermute | solution.py:24

commit v3 on v2

--- a/solution.py
+++ b/solution.py
@@ -203,7 +203,7 @@
     bias_ref[...] = whole[taps + split:taps + split + 1, :chans]
 
 
-GROUP = 4
+GROUP = 8
 
 
 def per_device(

time: 38.2 us -> 38.2 us (level)
  no operation moved by 1% of the time
where the time goes in v3:
time: 38.2 us; the launch traced here: 38 us
  starting transfers between devices  14.1 us (37%)
  waiting for transfers between devices  14.1 us (37%)
  Pallas kernels  6.94 us (18%)
  between operations  1.58 us (4%)
  local copies, waits for them, and re-layouts  1.12 us (3%)
    ppermute x12, starting transfers between devices, send(): lax.ppermute(x, MESH, [(index(*place), index(*target(*place))) for place...  14.1 us
    ppermute x12, waiting for transfers between devices, send(): lax.ppermute(x, MESH, [(index(*place), index(*target(*place))) for place...  14.1 us
    pallas_call x1, Pallas kernels, per_device(): pl.pallas_call(functools.partial(tile_kernel, norm=1.0 / (edge * edge)),...  5.68 us
    pallas_call x1, Pallas kernels, per_device(): pl.pallas_call(unpack_kernel, out_shape=(jax.ShapeDtypeStruct((3, 3, chan...  0.83 us
  transfers between devices with their start and end apart: 12, of which 9 were waited for; matrix products, arithmetic and copies ran while one was open for 2% of the time, Pallas kernels for 0%

profile of v3, /device:TPU:0, one launch (start us, length us, event | category | flops | bytes accessed | tf_op | source)
XLA Modules:
  0.0 38.0 jit_solution(2818036496116124674)
XLA Ops:
  1.4 0.2 copy-done.3
  1.8 0.4 %project.1 = (f32[72,128]{1,0:T(8,128)S(1)}, f32[72,128]{1,0:T(8,128)S(1)}, f32[8,128]{1,0:T(8,128)S(1)}) custom-call(f32[8,128]{1,0:T(8,128)S(1)} %zeros.1.zeros_ref, s32[1,1]{1,0:T(1,128)S(6)} %copy.21.kept_ref, bf16[128,640]{1,0:T(8,128)(2,1)S(1)} %copy-done.1, bf16[64,1280]{1,0:T(8,128)(2,1)S(1)} %bitcast.8, bf16[320,128]{1,0:T(8,128)(2,1)S(1)} %bitcast.10, ...), custom_call_target="tpu_custom_call" | custom-call | flops 2000000000 | bytes 1000 | tf_op jit(solution)/shard_map/project/pallas_call | solution.py:234
  2.2 4.0 %collective-permute-start.3 = (f32[8,128]{1,0:T(8,128)S(1)}, f32[8,128]{1,0:T(8,128)S(1)}, u32[]{:S(2)}, u32[]{:S(2)}) collective-permute-start(f32[8,128]{1,0:T(8,128)S(1)} %get-tuple-element.12), channel_id=1, source_target_pairs={{0,6},{1,7},{2,4},{3,5},{4,2},{5,3},{6,0},{7,1},{8,14},{9,15},{10,... | collective-permute-start | bytes 12296 | tf_op jit(solution)/shard_map/ppermute | solution.py:24
  6.2 0.4 %collective-permute-start.1 = (f32[72,128]{1,0:T(8,128)S(1)}, f32[72,128]{1,0:T(8,128)S(1)}, u32[]{:S(2)}, u32[]{:S(2)}) collective-permute-start(f32[72,128]{1,0:T(8,128)S(1)} %get-tuple-element.11), channel_id=1, source_target_pairs={{0,4},{1,5},{2,6},{3,7},{4,0},{5,1},{6,2},{7,3},{8,12},{9,13},{10,... | collective-permute-start | bytes 110600 | tf_op jit(solution)/shard_map/ppermute | solution.py:24
  6.7 1.2 %collective-permute-start = (f32[72,128]{1,0:T(8,128)S(1)}, f32[72,128]{1,0:T(8,128)S(1)}, u32[]{:S(2)}, u32[]{:S(2)}) collective-permute-start(f32[72,128]{1,0:T(8,128)S(1)} %get-tuple-element.10), channel_id=1, source_target_pairs={{0,2},{1,3},{2,0},{3,1},{4,6},{5,7},{6,4},{7,5},{8,10},{9,11},{10,... | collective-permute-start | bytes 110600 | tf_op jit(solution)/shard_map/ppermute | solution.py:24
  8.3 0.2 copy.18
  8.5 0.2 reshape.22.weight_ref
  8.7 0.6 %collective-permute-done.2 = f32[8,128]{1,0:T(8,128)S(1)} collective-permute-done((f32[8,128]{1,0:T(8,128)S(1)}, f32[8,128]{1,0:T(8,128)S(1)}, u32[]{:S(2)}, u32[]{:S(2)}) %collective-permute-start.2) | collective-permute-done | bytes 4128 | tf_op jit(solution)/shard_map/ppermute | solution.py:24
  9.3 1.0 %collective-permute-done.1 = f32[72,128]{1,0:T(8,128)S(1)} collective-permute-done((f32[72,128]{1,0:T(8,128)S(1)}, f32[72,128]{1,0:T(8,128)S(1)}, u32[]{:S(2)}, u32[]{:S(2)}) %collective-permute-start.1) | collective-permute-done | bytes 36896 | tf_op jit(solution)/shard_map/ppermute | solution.py:24
  10.4 2.7 %collective-permute-start.4 = (f32[72,128]{1,0:T(8,128)S(1)}, f32[72,128]{1,0:T(8,128)S(1)}, u32[]{:S(2)}, u32[]{:S(2)}) collective-permute-start(f32[72,128]{1,0:T(8,128)S(1)} %concatenate.20), channel_id=1, source_target_pairs={{0,9},{1,8},{2,11},{3,10},{4,13},{5,12},{6,15},{7,14},{8,1},{9,0},... | collective-permute-start | bytes 110600 | tf_op jit(solution)/shard_map/ppermute | solution.py:24
  13.2 2.5 %collective-permute-done.4 = f32[72,128]{1,0:T(8,128)S(1)} collective-permute-done((f32[72,128]{1,0:T(8,128)S(1)}, f32[72,128]{1,0:T(8,128)S(1)}, u32[]{:S(2)}, u32[]{:S(2)}) %collective-permute-start.4) | collective-permute-done | bytes 36896 | tf_op jit(solution)/shard_map/ppermute | solution.py:24
  15.8 5.7 %tile.1 = (f32[128,128]{1,0:T(8,128)}, f32[304,128]{1,0:T(8,128)S(1)}) custom-call(f32[64,128]{1,0:T(8,128)S(1)} %slice_add_fusion.2.row_ref, f32[64,128]{1,0:T(8,128)S(1)} %slice_add_fusion.col_ref, f32[16,128]{1,0:T(8,128)S(1)} %concatenate.23.misc_ref, f32[64,128]{1,0:T(8,128)S(1)} %maximum_convert_fusion.out_ref, f32[64,1]{1,0:T(8,128)S(1)} %copy.19.pbias_ref, ...), custom_call_target="tpu_custom_call" | custom-call | tf_op jit(solution)/shard_map/tile/pallas_call | solution.py:317
  21.5 0.1 collective-permute-start.6
  21.6 1.2 %collective-permute-done.6 = f32[152,128]{1,0:T(8,128)S(1)} collective-permute-done((f32[152,128]{1,0:T(8,128)S(1)}, f32[152,128]{1,0:T(8,128)S(1)}, u32[]{:S(2)}, u32[]{:S(2)}) %collective-permute-start.6) | collective-permute-done | bytes 77856 | tf_op jit(solution)/shard_map/ppermute | solution.py:24
  22.8 0.6 %collective-permute-start.9 = (f32[152,128]{1,0:T(8,128)S(1)}, f32[152,128]{1,0:T(8,128)S(1)}, u32[]{:S(2)}, u32[]{:S(2)}) collective-permute-start(f32[152,128]{1,0:T(8,128)S(1)} %dynamic-slice_add_fusion), channel_id=1, source_target_pairs={{0,6},{1,7},{2,4},{3,5},{4,2},{5,3},{6,0},{7,1},{8,14},{9,15},{10,... | collective-permute-start | bytes 233480 | tf_op jit(solution)/shard_map/ppermute | solution.py:24
  23.4 2.3 %collective-permute-start.8 = (f32[152,128]{1,0:T(8,128)S(1)}, f32[152,128]{1,0:T(8,128)S(1)}, u32[]{:S(2)}, u32[]{:S(2)}) collective-permute-start(f32[152,128]{1,0:T(8,128)S(1)} %dynamic-slice_add_fusion), channel_id=1, source_target_pairs={{0,4},{1,5},{2,6},{3,7},{4,0},{5,1},{6,2},{7,3},{8,12},{9,13},{10,... | collective-permute-start | bytes 233480 | tf_op jit(solution)/shard_map/ppermute | solution.py:24
  25.8 0.6 %collective-permute-start.7 = (f32[152,128]{1,0:T(8,128)S(1)}, f32[152,128]{1,0:T(8,128)S(1)}, u32[]{:S(2)}, u32[]{:S(2)}) collective-permute-start(f32[152,128]{1,0:T(8,128)S(1)} %dynamic-slice_add_fusion), channel_id=1, source_target_pairs={{0,2},{1,3},{2,0},{3,1},{4,6},{5,7},{6,4},{7,5},{8,10},{9,11},{10,... | collective-permute-start | bytes 233480 | tf_op jit(solution)/shard_map/ppermute | solution.py:24
  26.4 2.6 %collective-permute-done.9 = f32[152,128]{1,0:T(8,128)S(1)} collective-permute-done((f32[152,128]{1,0:T(8,128)S(1)}, f32[152,128]{1,0:T(8,128)S(1)}, u32[]{:S(2)}, u32[]{:S(2)}) %collective-permute-start.9) | collective-permute-done | bytes 77856 | tf_op jit(solution)/shard_map/ppermute | solution.py:24
  29.0 0.9 %collective-permute-done.8 = f32[152,128]{1,0:T(8,128)S(1)} collective-permute-done((f32[152,128]{1,0:T(8,128)S(1)}, f32[152,128]{1,0:T(8,128)S(1)}, u32[]{:S(2)}, u32[]{:S(2)}) %collective-permute-start.8) | collective-permute-done | bytes 77856 | tf_op jit(solution)/shard_map/ppermute | solution.py:24
  29.8 0.3 collective-permute-done.7
  30.2 1.9 %collective-permute-start.10 = (f32[152,128]{1,0:T(8,128)S(1)}, f32[152,128]{1,0:T(8,128)S(1)}, u32[]{:S(2)}, u32[]{:S(2)}) collective-permute-start(f32[152,128]{1,0:T(8,128)S(1)} %add_add_fusion), channel_id=1, source_target_pairs={{0,8},{1,9},{2,10},{3,11},{4,12},{5,13},{6,14},{7,15},{8,0},{9,1},... | collective-permute-start | bytes 233480 | tf_op jit(solution)/shard_map/ppermute | solution.py:24
  32.1 3.7 %collective-permute-done.10 = f32[152,128]{1,0:T(8,128)S(1)} collective-permute-done((f32[152,128]{1,0:T(8,128)S(1)}, f32[152,128]{1,0:T(8,128)S(1)}, u32[]{:S(2)}, u32[]{:S(2)}) %collective-permute-start.10) | collective-permute-done | bytes 77856 | tf_op jit(solution)/shard_map/ppermute | solution.py:24
  35.9 1.3 %collective-permute-done.11.other_ref = f32[152,128]{1,0:T(8,128)S(1)} collective-permute-done((f32[152,128]{1,0:T(8,128)S(1)}, f32[152,128]{1,0:T(8,128)S(1)}, u32[]{:S(2)}, u32[]{:S(2)}) %collective-permute-start.11) | collective-permute-done | bytes 77856 | tf_op jit(solution)/shard_map/ppermute | solution.py:24
  37.2 0.8 %unpack.1 = (f32[3,3,64,64]{3,2,1,0:T(8,128)}, f32[1,64]{1,0:T(1,128)}) custom-call(f32[152,128]{1,0:T(8,128)S(1)} %add.60.own_ref, f32[152,128]{1,0:T(8,128)S(1)} %collective-permute-done.11.other_ref), custom_call_target="tpu_custom_call" | custom-call | tf_op jit(solution)/shard_map/unpack/pallas_call | solution.py:350
  (52 shorter events, 1.0 us)
Async XLA Ops:
  0.6 0.9 %copy-start.3 = (bf16[1280,64]{0,1:T(8,128)(2,1)S(1)}, bf16[1280,64]{0,1:T(8,128)(2,1)}, u32[]{:S(2)}) copy-start(bf16[1280,64]{0,1:T(8,128)(2,1)} %param.13) | copy-start | bytes 491524
  0.6 1.0 %copy-start.2 = (bf16[1280,64]{0,1:T(8,128)(2,1)S(1)}, bf16[1280,64]{0,1:T(8,128)(2,1)}, u32[]{:S(2)}) copy-start(bf16[1280,64]{0,1:T(8,128)(2,1)} %param.12) | copy-start | bytes 491524
  0.7 1.0 %copy-start.4 = (bf16[128,320]{0,1:T(8,128)(2,1)S(1)}, bf16[128,320]{0,1:T(8,128)(2,1)}, u32[]{:S(2)}) copy-start(bf16[128,320]{0,1:T(8,128)(2,1)} %param.11) | copy-start | bytes 245764
  0.7 1.1 %copy-start.1 = (bf16[128,640]{1,0:T(8,128)(2,1)S(1)}, bf16[128,640]{1,0:T(8,128)(2,1)}, u32[]{:S(2)}) copy-start(bf16[128,640]{1,0:T(8,128)(2,1)} %row_ref.1) | copy-start | bytes 491524
  1.8 6.1 %copy-start.6 = (bf16[64,64]{1,0:T(8,128)(2,1)S(1)}, bf16[64,64]{1,0:T(8,128)(2,1)}, u32[]{:S(2)}) copy-start(bf16[64,64]{1,0:T(8,128)(2,1)} %param.14) | copy-start | bytes 24580
  1.8 6.3 %copy-start.7 = (f32[64]{0:T(128)S(1)}, f32[64]{0:T(128)}, u32[]{:S(2)}) copy-start(f32[64]{0:T(128)} %param.15) | copy-start | bytes 772
  1.8 6.4 %copy-start.8 = (f32[64]{0:T(128)S(1)}, f32[64]{0:T(128)}, u32[]{:S(2)}) copy-start(f32[64]{0:T(128)} %param.17) | copy-start | bytes 772
  1.8 6.5 %copy-start.5 = (bf16[3,3,64,64]{3,2,1,0:T(8,128)(2,1)S(1)}, bf16[3,3,64,64]{3,2,1,0:T(8,128)(2,1)}, u32[]{:S(2)}) copy-start(bf16[3,3,64,64]{3,2,1,0:T(8,128)(2,1)} %param.16) | copy-start | bytes 221188
  1.8 14.0 %copy-start = (bf16[64,128,128]{2,1,0:T(8,128)(2,1)S(1)}, bf16[64,128,128]{2,1,0:T(8,128)(2,1)}, u32[]{:S(2)}) copy-start(bf16[64,128,128]{2,1,0:T(8,128)(2,1)} %target_ref.1) | copy-start | bytes 6291460
  2.2 6.4 %collective-permute-start.3 = (f32[8,128]{1,0:T(8,128)S(1)}, f32[8,128]{1,0:T(8,128)S(1)}, u32[]{:S(2)}, u32[]{:S(2)}) collective-permute-start(f32[8,128]{1,0:T(8,128)S(1)} %get-tuple-element.12), channel_id=1, source_target_pairs={{0,6},{1,7},{2,4},{3,5},{4,2},{5,3},{6,0},{7,1},{8,14},{9,15},{10,... | collective-permute-start | bytes 12296 | tf_op jit(solution)/shard_map/ppermute | solution.py:24
  6.2 3.0 %collective-permute-start.2 = (f32[8,128]{1,0:T(8,128)S(1)}, f32[8,128]{1,0:T(8,128)S(1)}, u32[]{:S(2)}, u32[]{:S(2)}) collective-permute-start(f32[8,128]{1,0:T(8,128)S(1)} %get-tuple-element.12), channel_id=1, source_target_pairs={{0,3},{1,2},{2,1},{3,0},{4,7},{5,6},{6,5},{7,4},{8,11},{9,10},{10,... | collective-permute-start | bytes 12296 | tf_op jit(solution)/shard_map/ppermute | solution.py:24
  6.2 4.0 %collective-permute-start.1 = (f32[72,128]{1,0:T(8,128)S(1)}, f32[72,128]{1,0:T(8,128)S(1)}, u32[]{:S(2)}, u32[]{:S(2)}) collective-permute-start(f32[72,128]{1,0:T(8,128)S(1)} %get-tuple-element.11), channel_id=1, source_target_pairs={{0,4},{1,5},{2,6},{3,7},{4,0},{5,1},{6,2},{7,3},{8,12},{9,13},{10,... | collective-permute-start | bytes 110600 | tf_op jit(solution)/shard_map/ppermute | solution.py:24
  6.7 6.5 %collective-permute-start = (f32[72,128]{1,0:T(8,128)S(1)}, f32[72,128]{1,0:T(8,128)S(1)}, u32[]{:S(2)}, u32[]{:S(2)}) collective-permute-start(f32[72,128]{1,0:T(8,128)S(1)} %get-tuple-element.10), channel_id=1, source_target_pairs={{0,2},{1,3},{2,0},{3,1},{4,6},{5,7},{6,4},{7,5},{8,10},{9,11},{10,... | collective-permute-start | bytes 110600 | tf_op jit(solution)/shard_map/ppermute | solution.py:24
  10.3 2.9 %collective-permute-start.5 = (f32[8,128]{1,0:T(8,128)S(1)}, f32[8,128]{1,0:T(8,128)S(1)}, u32[]{:S(2)}, u32[]{:S(2)}) collective-permute-start(f32[8,128]{1,0:T(8,128)S(1)} %pad_maximum_fusion), channel_id=1, source_target_pairs={{0,1},{1,0},{2,3},{3,2},{4,5},{5,4},{6,7},{7,6},{8,9},{9,8},{10,11... | collective-permute-start | bytes 12296 | tf_op jit(solution)/shard_map/ppermute | solution.py:24
  10.4 5.3 %collective-permute-start.4 = (f32[72,128]{1,0:T(8,128)S(1)}, f32[72,128]{1,0:T(8,128)S(1)}, u32[]{:S(2)}, u32[]{:S(2)}) collective-permute-start(f32[72,128]{1,0:T(8,128)S(1)} %concatenate.20), channel_id=1, source_target_pairs={{0,9},{1,8},{2,11},{3,10},{4,13},{5,12},{6,15},{7,14},{8,1},{9,0},... | collective-permute-start | bytes 110600 | tf_op jit(solution)/shard_map/ppermute | solution.py:24
  21.5 1.3 %collective-permute-start.6 = (f32[152,128]{1,0:T(8,128)S(1)}, f32[152,128]{1,0:T(8,128)S(1)}, u32[]{:S(2)}, u32[]{:S(2)}) collective-permute-start(f32[152,128]{1,0:T(8,128)S(1)} %constant_dynamic-slice_fusion), channel_id=1, source_target_pairs={{0,1},{1,0},{2,3},{3,2},{4,5},{5,4},{6,7},{7,6},{8,9},{9,8},{10,11... | collective-permute-start | bytes 233480 | tf_op jit(solution)/shard_map/ppermute | solution.py:24
  22.8 6.2 %collective-permute-start.9 = (f32[152,128]{1,0:T(8,128)S(1)}, f32[152,128]{1,0:T(8,128)S(1)}, u32[]{:S(2)}, u32[]{:S(2)}) collective-permute-start(f32[152,128]{1,0:T(8,128)S(1)} %dynamic-slice_add_fusion), channel_id=1, source_target_pairs={{0,6},{1,7},{2,4},{3,5},{4,2},{5,3},{6,0},{7,1},{8,14},{9,15},{10,... | collective-permute-start | bytes 233480 | tf_op jit(solution)/shard_map/ppermute | solution.py:24
  23.4 6.4 %collective-permute-start.8 = (f32[152,128]{1,0:T(8,128)S(1)}, f32[152,128]{1,0:T(8,128)S(1)}, u32[]{:S(2)}, u32[]{:S(2)}) collective-permute-start(f32[152,128]{1,0:T(8,128)S(1)} %dynamic-slice_add_fusion), channel_id=1, source_target_pairs={{0,4},{1,5},{2,6},{3,7},{4,0},{5,1},{6,2},{7,3},{8,12},{9,13},{10,... | collective-permute-start | bytes 233480 | tf_op jit(solution)/shard_map/ppermute | solution.py:24
  25.8 4.4 %collective-permute-start.7 = (f32[152,128]{1,0:T(8,128)S(1)}, f32[152,128]{1,0:T(8,128)S(1)}, u32[]{:S(2)}, u32[]{:S(2)}) collective-permute-start(f32[152,128]{1,0:T(8,128)S(1)} %dynamic-slice_add_fusion), channel_id=1, source_target_pairs={{0,2},{1,3},{2,0},{3,1},{4,6},{5,7},{6,4},{7,5},{8,10},{9,11},{10,... | collective-permute-start | bytes 233480 | tf_op jit(solution)/shard_map/ppermute | solution.py:24
  30.2 5.6 %collective-permute-start.10 = (f32[152,128]{1,0:T(8,128)S(1)}, f32[152,128]{1,0:T(8,128)S(1)}, u32[]{:S(2)}, u32[]{:S(2)}) collective-permute-start(f32[152,128]{1,0:T(8,128)S(1)} %add_add_fusion), channel_id=1, source_target_pairs={{0,8},{1,9},{2,10},{3,11},{4,12},{5,13},{6,14},{7,15},{8,0},{9,1},... | collective-permute-start | bytes 233480 | tf_op jit(solution)/shard_map/ppermute | solution.py:24
  35.8 1.3 %collective-permute-start.11 = (f32[152,128]{1,0:T(8,128)S(1)}, f32[152,128]{1,0:T(8,128)S(1)}, u32[]{:S(2)}, u32[]{:S(2)}) collective-permute-start(f32[152,128]{1,0:T(8,128)S(1)} %add.60.own_ref), channel_id=1, source_target_pairs={{0,1},{1,0},{2,3},{3,2},{4,5},{5,4},{6,7},{7,6},{8,9},{9,8},{10,11... | collective-permute-start | bytes 233480 | tf_op jit(solution)/shard_map/ppermute | solution.py:24

commit v4 on v2

--- a/solution.py
+++ b/solution.py
@@ -157,8 +157,11 @@
     cbias = jnp.broadcast_to(cbias_ref[...], (chans, width))
     keep = jnp.concatenate([misc_ref[4:5, :]] * 2, axis=1)
     bias_sum = jnp.zeros((chans, width), F32)
+    joined = 3 if pairs % 3 == 0 else 1
     for e in range(pairs):
-        part = jnp.dot(weight_ref[...], hid[:, e * width:(e + 1) * width], preferred_element_type=F32)
+        if e % joined == 0:
+            parts = jnp.dot(weight_ref[...], hid[:, e * width:(e + joined) * width], preferred_element_type=F32)
+        part = parts[:, e % joined * width:(e % joined + 1) * width]
         m = e - 2
         if m >= 0:
             target = jnp.concatenate([turned_target[2 * m], turned_target[2 * m + 1]], axis=1).astype(F32)

time: 38.2 us -> 38.2 us (level)
  no operation moved by 1% of the time
where the time goes in v4:
time: 38.2 us; the launch traced here: 38 us
  starting transfers between devices  14.1 us (37%)
  waiting for transfers between devices  14.1 us (37%)
  Pallas kernels  6.97 us (18%)
  between operations  1.58 us (4%)
  local copies, waits for them, and re-layouts  1.12 us (3%)
    ppermute x12, starting transfers between devices, send(): lax.ppermute(x, MESH, [(index(*place), index(*target(*place))) for place...  14.1 us
    ppermute x12, waiting for transfers between devices, send(): lax.ppermute(x, MESH, [(index(*place), index(*target(*place))) for place...  14.1 us
    pallas_call x1, Pallas kernels, per_device(): pl.pallas_call(functools.partial(tile_kernel, norm=1.0 / (edge * edge)),...  5.72 us
    pallas_call x1, Pallas kernels, per_device(): pl.pallas_call(unpack_kernel, out_shape=(jax.ShapeDtypeStruct((3, 3, chan...  0.83 us
  transfers between devices with their start and end apart: 12, of which 9 were waited for; matrix products, arithmetic and copies ran while one was open for 2% of the time, Pallas kernels for 0%

profile of v4, /device:TPU:0, one launch (start us, length us, event | category | flops | bytes accessed | tf_op | source)
XLA Modules:
  0.0 38.0 jit_solution(5818063265682779262)
XLA Ops:
  1.4 0.2 copy-done.3
  1.8 0.4 %project.1 = (f32[72,128]{1,0:T(8,128)S(1)}, f32[72,128]{1,0:T(8,128)S(1)}, f32[8,128]{1,0:T(8,128)S(1)}) custom-call(f32[8,128]{1,0:T(8,128)S(1)} %zeros.1.zeros_ref, s32[1,1]{1,0:T(1,128)S(6)} %copy.21.kept_ref, bf16[128,640]{1,0:T(8,128)(2,1)S(1)} %copy-done.1, bf16[64,1280]{1,0:T(8,128)(2,1)S(1)} %bitcast.8, bf16[320,128]{1,0:T(8,128)(2,1)S(1)} %bitcast.10, ...), custom_call_target="tpu_custom_call" | custom-call | flops 2000000000 | bytes 1000 | tf_op jit(solution)/shard_map/project/pallas_call | solution.py:237
  2.2 4.0 %collective-permute-start.3 = (f32[8,128]{1,0:T(8,128)S(1)}, f32[8,128]{1,0:T(8,128)S(1)}, u32[]{:S(2)}, u32[]{:S(2)}) collective-permute-start(f32[8,128]{1,0:T(8,128)S(1)} %get-tuple-element.12), channel_id=1, source_target_pairs={{0,6},{1,7},{2,4},{3,5},{4,2},{5,3},{6,0},{7,1},{8,14},{9,15},{10,... | collective-permute-start | bytes 12296 | tf_op jit(solution)/shard_map/ppermute | solution.py:24
  6.2 0.4 %collective-permute-start.1 = (f32[72,128]{1,0:T(8,128)S(1)}, f32[72,128]{1,0:T(8,128)S(1)}, u32[]{:S(2)}, u32[]{:S(2)}) collective-permute-start(f32[72,128]{1,0:T(8,128)S(1)} %get-tuple-element.11), channel_id=1, source_target_pairs={{0,4},{1,5},{2,6},{3,7},{4,0},{5,1},{6,2},{7,3},{8,12},{9,13},{10,... | collective-permute-start | bytes 110600 | tf_op jit(solution)/shard_map/ppermute | solution.py:24
  6.7 1.2 %collective-permute-start = (f32[72,128]{1,0:T(8,128)S(1)}, f32[72,128]{1,0:T(8,128)S(1)}, u32[]{:S(2)}, u32[]{:S(2)}) collective-permute-start(f32[72,128]{1,0:T(8,128)S(1)} %get-tuple-element.10), channel_id=1, source_target_pairs={{0,2},{1,3},{2,0},{3,1},{4,6},{5,7},{6,4},{7,5},{8,10},{9,11},{10,... | collective-permute-start | bytes 110600 | tf_op jit(solution)/shard_map/ppermute | solution.py:24
  8.3 0.2 copy.18
  8.5 0.2 reshape.22.weight_ref
  8.7 0.6 %collective-permute-done.2 = f32[8,128]{1,0:T(8,128)S(1)} collective-permute-done((f32[8,128]{1,0:T(8,128)S(1)}, f32[8,128]{1,0:T(8,128)S(1)}, u32[]{:S(2)}, u32[]{:S(2)}) %collective-permute-start.2) | collective-permute-done | bytes 4128 | tf_op jit(solution)/shard_map/ppermute | solution.py:24
  9.3 1.0 %collective-permute-done.1 = f32[72,128]{1,0:T(8,128)S(1)} collective-permute-done((f32[72,128]{1,0:T(8,128)S(1)}, f32[72,128]{1,0:T(8,128)S(1)}, u32[]{:S(2)}, u32[]{:S(2)}) %collective-permute-start.1) | collective-permute-done | bytes 36896 | tf_op jit(solution)/shard_map/ppermute | solution.py:24
  10.4 2.7 %collective-permute-start.4 = (f32[72,128]{1,0:T(8,128)S(1)}, f32[72,128]{1,0:T(8,128)S(1)}, u32[]{:S(2)}, u32[]{:S(2)}) collective-permute-start(f32[72,128]{1,0:T(8,128)S(1)} %concatenate.20), channel_id=1, source_target_pairs={{0,9},{1,8},{2,11},{3,10},{4,13},{5,12},{6,15},{7,14},{8,1},{9,0},... | collective-permute-start | bytes 110600 | tf_op jit(solution)/shard_map/ppermute | solution.py:24
  13.2 2.5 %collective-permute-done.4 = f32[72,128]{1,0:T(8,128)S(1)} collective-permute-done((f32[72,128]{1,0:T(8,128)S(1)}, f32[72,128]{1,0:T(8,128)S(1)}, u32[]{:S(2)}, u32[]{:S(2)}) %collective-permute-start.4) | collective-permute-done | bytes 36896 | tf_op jit(solution)/shard_map/ppermute | solution.py:24
  15.8 5.7 %tile.1 = (f32[128,128]{1,0:T(8,128)}, f32[304,128]{1,0:T(8,128)S(1)}) custom-call(f32[64,128]{1,0:T(8,128)S(1)} %slice_add_fusion.2.row_ref, f32[64,128]{1,0:T(8,128)S(1)} %slice_add_fusion.col_ref, f32[16,128]{1,0:T(8,128)S(1)} %concatenate.23.misc_ref, f32[64,128]{1,0:T(8,128)S(1)} %maximum_convert_fusion.out_ref, f32[64,1]{1,0:T(8,128)S(1)} %copy.19.pbias_ref, ...), custom_call_target="tpu_custom_call" | custom-call | tf_op jit(solution)/shard_map/tile/pallas_call | solution.py:320
  21.5 0.1 collective-permute-start.6
  21.7 1.2 %collective-permute-done.6 = f32[152,128]{1,0:T(8,128)S(1)} collective-permute-done((f32[152,128]{1,0:T(8,128)S(1)}, f32[152,128]{1,0:T(8,128)S(1)}, u32[]{:S(2)}, u32[]{:S(2)}) %collective-permute-start.6) | collective-permute-done | bytes 77856 | tf_op jit(solution)/shard_map/ppermute | solution.py:24
  22.8 0.6 %collective-permute-start.9 = (f32[152,128]{1,0:T(8,128)S(1)}, f32[152,128]{1,0:T(8,128)S(1)}, u32[]{:S(2)}, u32[]{:S(2)}) collective-permute-start(f32[152,128]{1,0:T(8,128)S(1)} %dynamic-slice_add_fusion), channel_id=1, source_target_pairs={{0,6},{1,7},{2,4},{3,5},{4,2},{5,3},{6,0},{7,1},{8,14},{9,15},{10,... | collective-permute-start | bytes 233480 | tf_op jit(solution)/shard_map/ppermute | solution.py:24
  23.5 2.3 %collective-permute-start.8 = (f32[152,128]{1,0:T(8,128)S(1)}, f32[152,128]{1,0:T(8,128)S(1)}, u32[]{:S(2)}, u32[]{:S(2)}) collective-permute-start(f32[152,128]{1,0:T(8,128)S(1)} %dynamic-slice_add_fusion), channel_id=1, source_target_pairs={{0,4},{1,5},{2,6},{3,7},{4,0},{5,1},{6,2},{7,3},{8,12},{9,13},{10,... | collective-permute-start | bytes 233480 | tf_op jit(solution)/shard_map/ppermute | solution.py:24
  25.8 0.6 %collective-permute-start.7 = (f32[152,128]{1,0:T(8,128)S(1)}, f32[152,128]{1,0:T(8,128)S(1)}, u32[]{:S(2)}, u32[]{:S(2)}) collective-permute-start(f32[152,128]{1,0:T(8,128)S(1)} %dynamic-slice_add_fusion), channel_id=1, source_target_pairs={{0,2},{1,3},{2,0},{3,1},{4,6},{5,7},{6,4},{7,5},{8,10},{9,11},{10,... | collective-permute-start | bytes 233480 | tf_op jit(solution)/shard_map/ppermute | solution.py:24
  26.4 2.6 %collective-permute-done.9 = f32[152,128]{1,0:T(8,128)S(1)} collective-permute-done((f32[152,128]{1,0:T(8,128)S(1)}, f32[152,128]{1,0:T(8,128)S(1)}, u32[]{:S(2)}, u32[]{:S(2)}) %collective-permute-start.9) | collective-permute-done | bytes 77856 | tf_op jit(solution)/shard_map/ppermute | solution.py:24
  29.0 0.9 %collective-permute-done.8 = f32[152,128]{1,0:T(8,128)S(1)} collective-permute-done((f32[152,128]{1,0:T(8,128)S(1)}, f32[152,128]{1,0:T(8,128)S(1)}, u32[]{:S(2)}, u32[]{:S(2)}) %collective-permute-start.8) | collective-permute-done | bytes 77856 | tf_op jit(solution)/shard_map/ppermute | solution.py:24
  29.9 0.3 collective-permute-done.7
  30.2 1.9 %collective-permute-start.10 = (f32[152,128]{1,0:T(8,128)S(1)}, f32[152,128]{1,0:T(8,128)S(1)}, u32[]{:S(2)}, u32[]{:S(2)}) collective-permute-start(f32[152,128]{1,0:T(8,128)S(1)} %add_add_fusion), channel_id=1, source_target_pairs={{0,8},{1,9},{2,10},{3,11},{4,12},{5,13},{6,14},{7,15},{8,0},{9,1},... | collective-permute-start | bytes 233480 | tf_op jit(solution)/shard_map/ppermute | solution.py:24
  32.1 3.7 %collective-permute-done.10 = f32[152,128]{1,0:T(8,128)S(1)} collective-permute-done((f32[152,128]{1,0:T(8,128)S(1)}, f32[152,128]{1,0:T(8,128)S(1)}, u32[]{:S(2)}, u32[]{:S(2)}) %collective-permute-start.10) | collective-permute-done | bytes 77856 | tf_op jit(solution)/shard_map/ppermute | solution.py:24
  36.0 1.3 %collective-permute-done.11.other_ref = f32[152,128]{1,0:T(8,128)S(1)} collective-permute-done((f32[152,128]{1,0:T(8,128)S(1)}, f32[152,128]{1,0:T(8,128)S(1)}, u32[]{:S(2)}, u32[]{:S(2)}) %collective-permute-start.11) | collective-permute-done | bytes 77856 | tf_op jit(solution)/shard_map/ppermute | solution.py:24
  37.2 0.8 %unpack.1 = (f32[3,3,64,64]{3,2,1,0:T(8,128)}, f32[1,64]{1,0:T(1,128)}) custom-call(f32[152,128]{1,0:T(8,128)S(1)} %add.60.own_ref, f32[152,128]{1,0:T(8,128)S(1)} %collective-permute-done.11.other_ref), custom_call_target="tpu_custom_call" | custom-call | tf_op jit(solution)/shard_map/unpack/pallas_call | solution.py:353
  (52 shorter events, 1.0 us)
Async XLA Ops:
  0.6 0.9 %copy-start.3 = (bf16[1280,64]{0,1:T(8,128)(2,1)S(1)}, bf16[1280,64]{0,1:T(8,128)(2,1)}, u32[]{:S(2)}) copy-start(bf16[1280,64]{0,1:T(8,128)(2,1)} %param.13) | copy-start | bytes 491524
  0.6 1.0 %copy-start.2 = (bf16[1280,64]{0,1:T(8,128)(2,1)S(1)}, bf16[1280,64]{0,1:T(8,128)(2,1)}, u32[]{:S(2)}) copy-start(bf16[1280,64]{0,1:T(8,128)(2,1)} %param.12) | copy-start | bytes 491524
  0.7 1.0 %copy-start.4 = (bf16[128,320]{0,1:T(8,128)(2,1)S(1)}, bf16[128,320]{0,1:T(8,128)(2,1)}, u32[]{:S(2)}) copy-start(bf16[128,320]{0,1:T(8,128)(2,1)} %param.11) | copy-start | bytes 245764
  0.7 1.1 %copy-start.1 = (bf16[128,640]{1,0:T(8,128)(2,1)S(1)}, bf16[128,640]{1,0:T(8,128)(2,1)}, u32[]{:S(2)}) copy-start(bf16[128,640]{1,0:T(8,128)(2,1)} %row_ref.1) | copy-start | bytes 491524
  1.8 6.1 %copy-start.6 = (bf16[64,64]{1,0:T(8,128)(2,1)S(1)}, bf16[64,64]{1,0:T(8,128)(2,1)}, u32[]{:S(2)}) copy-start(bf16[64,64]{1,0:T(8,128)(2,1)} %param.14) | copy-start | bytes 24580
  1.8 6.3 %copy-start.7 = (f32[64]{0:T(128)S(1)}, f32[64]{0:T(128)}, u32[]{:S(2)}) copy-start(f32[64]{0:T(128)} %param.15) | copy-start | bytes 772
  1.8 6.4 %copy-start.8 = (f32[64]{0:T(128)S(1)}, f32[64]{0:T(128)}, u32[]{:S(2)}) copy-start(f32[64]{0:T(128)} %param.17) | copy-start | bytes 772
  1.8 6.5 %copy-start.5 = (bf16[3,3,64,64]{3,2,1,0:T(8,128)(2,1)S(1)}, bf16[3,3,64,64]{3,2,1,0:T(8,128)(2,1)}, u32[]{:S(2)}) copy-start(bf16[3,3,64,64]{3,2,1,0:T(8,128)(2,1)} %param.16) | copy-start | bytes 221188
  1.8 14.0 %copy-start = (bf16[64,128,128]{2,1,0:T(8,128)(2,1)S(1)}, bf16[64,128,128]{2,1,0:T(8,128)(2,1)}, u32[]{:S(2)}) copy-start(bf16[64,128,128]{2,1,0:T(8,128)(2,1)} %target_ref.1) | copy-start | bytes 6291460
  2.2 6.4 %collective-permute-start.3 = (f32[8,128]{1,0:T(8,128)S(1)}, f32[8,128]{1,0:T(8,128)S(1)}, u32[]{:S(2)}, u32[]{:S(2)}) collective-permute-start(f32[8,128]{1,0:T(8,128)S(1)} %get-tuple-element.12), channel_id=1, source_target_pairs={{0,6},{1,7},{2,4},{3,5},{4,2},{5,3},{6,0},{7,1},{8,14},{9,15},{10,... | collective-permute-start | bytes 12296 | tf_op jit(solution)/shard_map/ppermute | solution.py:24
  6.2 3.0 %collective-permute-start.2 = (f32[8,128]{1,0:T(8,128)S(1)}, f32[8,128]{1,0:T(8,128)S(1)}, u32[]{:S(2)}, u32[]{:S(2)}) collective-permute-start(f32[8,128]{1,0:T(8,128)S(1)} %get-tuple-element.12), channel_id=1, source_target_pairs={{0,3},{1,2},{2,1},{3,0},{4,7},{5,6},{6,5},{7,4},{8,11},{9,10},{10,... | collective-permute-start | bytes 12296 | tf_op jit(solution)/shard_map/ppermute | solution.py:24
  6.2 4.0 %collective-permute-start.1 = (f32[72,128]{1,0:T(8,128)S(1)}, f32[72,128]{1,0:T(8,128)S(1)}, u32[]{:S(2)}, u32[]{:S(2)}) collective-permute-start(f32[72,128]{1,0:T(8,128)S(1)} %get-tuple-element.11), channel_id=1, source_target_pairs={{0,4},{1,5},{2,6},{3,7},{4,0},{5,1},{6,2},{7,3},{8,12},{9,13},{10,... | collective-permute-start | bytes 110600 | tf_op jit(solution)/shard_map/ppermute | solution.py:24
  6.7 6.5 %collective-permute-start = (f32[72,128]{1,0:T(8,128)S(1)}, f32[72,128]{1,0:T(8,128)S(1)}, u32[]{:S(2)}, u32[]{:S(2)}) collective-permute-start(f32[72,128]{1,0:T(8,128)S(1)} %get-tuple-element.10), channel_id=1, source_target_pairs={{0,2},{1,3},{2,0},{3,1},{4,6},{5,7},{6,4},{7,5},{8,10},{9,11},{10,... | collective-permute-start | bytes 110600 | tf_op jit(solution)/shard_map/ppermute | solution.py:24
  10.3 2.9 %collective-permute-start.5 = (f32[8,128]{1,0:T(8,128)S(1)}, f32[8,128]{1,0:T(8,128)S(1)}, u32[]{:S(2)}, u32[]{:S(2)}) collective-permute-start(f32[8,128]{1,0:T(8,128)S(1)} %pad_maximum_fusion), channel_id=1, source_target_pairs={{0,1},{1,0},{2,3},{3,2},{4,5},{5,4},{6,7},{7,6},{8,9},{9,8},{10,11... | collective-permute-start | bytes 12296 | tf_op jit(solution)/shard_map/ppermute | solution.py:24
  10.4 5.3 %collective-permute-start.4 = (f32[72,128]{1,0:T(8,128)S(1)}, f32[72,128]{1,0:T(8,128)S(1)}, u32[]{:S(2)}, u32[]{:S(2)}) collective-permute-start(f32[72,128]{1,0:T(8,128)S(1)} %concatenate.20), channel_id=1, source_target_pairs={{0,9},{1,8},{2,11},{3,10},{4,13},{5,12},{6,15},{7,14},{8,1},{9,0},... | collective-permute-start | bytes 110600 | tf_op jit(solution)/shard_map/ppermute | solution.py:24
  21.5 1.3 %collective-permute-start.6 = (f32[152,128]{1,0:T(8,128)S(1)}, f32[152,128]{1,0:T(8,128)S(1)}, u32[]{:S(2)}, u32[]{:S(2)}) collective-permute-start(f32[152,128]{1,0:T(8,128)S(1)} %constant_dynamic-slice_fusion), channel_id=1, source_target_pairs={{0,1},{1,0},{2,3},{3,2},{4,5},{5,4},{6,7},{7,6},{8,9},{9,8},{10,11... | collective-permute-start | bytes 233480 | tf_op jit(solution)/shard_map/ppermute | solution.py:24
  22.8 6.2 %collective-permute-start.9 = (f32[152,128]{1,0:T(8,128)S(1)}, f32[152,128]{1,0:T(8,128)S(1)}, u32[]{:S(2)}, u32[]{:S(2)}) collective-permute-start(f32[152,128]{1,0:T(8,128)S(1)} %dynamic-slice_add_fusion), channel_id=1, source_target_pairs={{0,6},{1,7},{2,4},{3,5},{4,2},{5,3},{6,0},{7,1},{8,14},{9,15},{10,... | collective-permute-start | bytes 233480 | tf_op jit(solution)/shard_map/ppermute | solution.py:24
  23.5 6.4 %collective-permute-start.8 = (f32[152,128]{1,0:T(8,128)S(1)}, f32[152,128]{1,0:T(8,128)S(1)}, u32[]{:S(2)}, u32[]{:S(2)}) collective-permute-start(f32[152,128]{1,0:T(8,128)S(1)} %dynamic-slice_add_fusion), channel_id=1, source_target_pairs={{0,4},{1,5},{2,6},{3,7},{4,0},{5,1},{6,2},{7,3},{8,12},{9,13},{10,... | collective-permute-start | bytes 233480 | tf_op jit(solution)/shard_map/ppermute | solution.py:24
  25.8 4.4 %collective-permute-start.7 = (f32[152,128]{1,0:T(8,128)S(1)}, f32[152,128]{1,0:T(8,128)S(1)}, u32[]{:S(2)}, u32[]{:S(2)}) collective-permute-start(f32[152,128]{1,0:T(8,128)S(1)} %dynamic-slice_add_fusion), channel_id=1, source_target_pairs={{0,2},{1,3},{2,0},{3,1},{4,6},{5,7},{6,4},{7,5},{8,10},{9,11},{10,... | collective-permute-start | bytes 233480 | tf_op jit(solution)/shard_map/ppermute | solution.py:24
  30.2 5.6 %collective-permute-start.10 = (f32[152,128]{1,0:T(8,128)S(1)}, f32[152,128]{1,0:T(8,128)S(1)}, u32[]{:S(2)}, u32[]{:S(2)}) collective-permute-start(f32[152,128]{1,0:T(8,128)S(1)} %add_add_fusion), channel_id=1, source_target_pairs={{0,8},{1,9},{2,10},{3,11},{4,12},{5,13},{6,14},{7,15},{8,0},{9,1},... | collective-permute-start | bytes 233480 | tf_op jit(solution)/shard_map/ppermute | solution.py:24
  35.9 1.3 %collective-permute-start.11 = (f32[152,128]{1,0:T(8,128)S(1)}, f32[152,128]{1,0:T(8,128)S(1)}, u32[]{:S(2)}, u32[]{:S(2)}) collective-permute-start(f32[152,128]{1,0:T(8,128)S(1)} %add.60.own_ref), channel_id=1, source_target_pairs={{0,1},{1,0},{2,3},{3,2},{4,5},{5,4},{6,7},{7,6},{8,9},{9,8},{10,11... | collective-permute-start | bytes 233480 | tf_op jit(solution)/shard_map/ppermute | solution.py:24
